TPU v7x, 128 devices: a whole 4x4x4 slice. The times are simulated.
128 devices in a mesh: section: 2 (over core), dp: 64 (over y, z, x).
Axes of the slice: x: 4, y: 4, z: 4, core: 2. Of those that a mesh axis runs over, the one named last changes fastest.
Arguments:
- tokens: bfloat16 [2, 2, 64, 256, 512], P('section', None, 'dp'), may hold values from -16 to 16
- cotangent: bfloat16 [2, 2, 64, 256, 512], P('section', None, 'dp'), may hold values from -6 to 6
- source_lengths: int32 [2, 64, 8], P(None, 'dp'), may hold values from 1 to 128, 256 in all within a row
- target_segments: int32 [2, 64, 256], P(None, 'dp'), may hold values from 0 to 7, never falling along the last dimension, each value on 1 to 128 neighbouring positions
- self_in: bfloat16 [2, 512, 1536], P('section'), may hold values from -0.25 to 0.25
- self_out: bfloat16 [2, 512, 512], P('section'), may hold values from -1.5 to 1.5
- cross_weight: bfloat16 [2, 512, 1024], P('section'), may hold values from -0.625 to 0.625
- hidden_in: bfloat16 [2, 512, 2048], P('section'), may hold values from -0.25 to 0.25
- hidden_out: bfloat16 [2, 2048, 512], P('section'), may hold values from -0.125 to 0.125
- norm_params: float32 [2, 6, 512], P('section'), may hold values from -1.2 to 1.6, as said below
Outputs:
- layer_out: bfloat16 [2, 2, 64, 256, 512], P('section', None, 'dp')
- token_grads: float32 [2, 2, 64, 256, 512], P('section', None, 'dp')
- grad_self_in: float32 [2, 512, 1536], P('section', 'dp')
- grad_self_out: float32 [2, 512, 512], P('section', 'dp')
- grad_cross: float32 [2, 512, 1024], P('section', 'dp')
- grad_hidden_in: float32 [2, 512, 2048], P('section', 'dp')
- grad_hidden_out: float32 [2, 2048, 512], P('section', 'dp')
- grad_norms: float32 [2, 6, 512], P('section', None, 'dp')
Inputs may be any that keep to these rules, and one draw needn't show every extreme that they name: `source_lengths`: the 8 lengths of each row sum to 256; the longest document of each row has exactly 128 tokens. `target_segments`: along each row the numbers never fall; each of 0 to 7 appears on 1 to 128 positions, one of them on exactly 128. `norm_params`: gains are positive.
All inputs are finite; a program needn't handle non-finite values.
Results may differ from a plain program's by a relative error of at most 0.017.
Values may be sent and summed in bfloat16 or wider, within the bound.
A program may use at most 320 MiB of HBM per device.

v0:
```python
import functools
import jax
import jax.numpy as jnp
from jax import lax
from jax.experimental import pallas as pl
from jax.experimental.pallas import tpu as pltpu
from jax.sharding import PartitionSpec as P

HEADS = 8
D = 512
FF = 2048
ROW = 256
NSEG = 8
UNITS = 29
ROWS_OUT = UNITS * 16
root_half = 0.7071067811865476
inverse_root = 0.3989422804014327
F32 = jnp.float32
BF16 = jnp.bfloat16


def dot(a, b):
    return lax.dot_general(a, b, (((1,), (0,)), ((), ())), preferred_element_type=F32)


def dot_nt(a, b):
    return lax.dot_general(a, b, (((1,), (1,)), ((), ())), preferred_element_type=F32)


def dot_tn(a, b):
    return lax.dot_general(a, b, (((0,), (0,)), ((), ())), preferred_element_type=F32)


def sides(factor):
    lane = lax.broadcasted_iota(jnp.int32, (1, 128), 1)
    low = jnp.where(lane < 64, factor, 0.0).astype(BF16)
    high = jnp.where(lane < 64, 0.0, factor).astype(BF16)
    return (low, high)


def attend(query, key, value, bias, shares, context):
    scaled, plain = sides(0.125), sides(1.0)
    for pair in range(HEADS // 2):
        q, k, v = query(pair), key(pair), value(pair)
        total = None
        for side in range(2):
            scores = dot_nt(q * scaled[side], k) + bias[...]
            expval = jnp.exp(scores - jnp.max(scores, -1, keepdims=True))
            share = (expval * (1.0 / jnp.sum(expval, -1, keepdims=True))).astype(BF16)
            shares[2 * pair + side] = share
            part = dot(share, v * plain[side])
            total = part if total is None else total + part
        context[:, 128 * pair : 128 * pair + 128] = total.astype(BF16)


def attend_back(query, key, value, shares, context, grad_context, put_query, put_key, put_value):
    scaled, plain = sides(0.125), sides(1.0)
    for pair in range(HEADS // 2):
        q, k, v = query(pair), key(pair), value(pair)
        columns = slice(128 * pair, 128 * pair + 128)
        g = grad_context[:, columns]
        along = g.astype(F32) * context[:, columns].astype(F32)
        grads = [None, None, None]
        for side in range(2):
            share = shares[2 * pair + side]
            mine = g * plain[side]
            delta = jnp.sum(along * plain[side].astype(F32), -1, keepdims=True)
            ds = (share.astype(F32) * (dot_nt(mine, v) - delta)).astype(BF16)
            parts = (dot(ds, k * scaled[side]), dot_tn(ds, q * scaled[side]), dot_tn(share, mine))
            grads = [p if t is None else t + p for t, p in zip(grads, parts)]
        for put, grad in zip((put_query, put_key, put_value), grads):
            put(pair, grad.astype(BF16))


def mean(values):
    return jnp.sum(values, -1, keepdims=True) * (1.0 / D)


def norm(values, params, which, normed, scale):
    center = values - mean(values)
    inverse = lax.rsqrt(mean(center * center) + 1e-05)
    result = center * inverse
    normed[...] = result
    scale[...] = inverse
    return result * params[2 * which : 2 * which + 1, :] + params[2 * which + 1 : 2 * which + 2, :]


def norm_back(gradient, params, which, normed, scale, grad_norms):
    n = normed[...]
    grad_norms[2 * which : 2 * which + 1, :] = jnp.sum(gradient * n, 0, keepdims=True)
    grad_norms[2 * which + 1 : 2 * which + 2, :] = jnp.sum(gradient, 0, keepdims=True)
    scaled = gradient * params[2 * which : 2 * which + 1, :]
    return scale[...] * (scaled - mean(scaled) - n * mean(scaled * n))


def pack(packed, unit, value):
    shards = value.shape[0] // 8
    blocks = value.reshape(shards, 8, value.shape[1])
    for i in range(value.shape[1] // 256):
        two = jnp.concatenate([blocks[:, :, 256 * i : 256 * i + 128], blocks[:, :, 256 * i + 128 : 256 * i + 256]], 1)
        packed[:, 16 * (unit + i) : 16 * (unit + i) + 16, :] = two.astype(BF16)


def pack_tall(packed, unit, first, value):
    blocks = value.reshape(16, 4, 8, 512)
    for r in range(4):
        for i in range(2):
            two = jnp.concatenate([blocks[:, r, :, 256 * i : 256 * i + 128], blocks[:, r, :, 256 * i + 128 : 256 * i + 256]], 1)
            at = 16 * (unit + 2 * r + i)
            packed[first : first + 16, at : at + 16, :] = two.astype(BF16)


def pack_norms(packed, grad_norms):
    turned = jnp.concatenate([grad_norms[...], jnp.zeros((120, 512), F32)], 0).T
    tiles = turned.reshape(64, 8, 128)
    packed[:, 448:464, :] = jnp.concatenate([tiles, jnp.zeros((64, 8, 128), F32)], 1).astype(BF16)


SELF_IN, SELF_OUT, CROSS, HIDDEN_IN, HIDDEN_OUT = 0, 6, 8, 12, 20


def columns_of(ref, first):
    return lambda pair: ref[:, first + 128 * pair : first + 128 * pair + 128]


def putter(ref, first):
    def put(pair, value):
        ref[:, first + 128 * pair : first + 128 * pair + 128] = value
    return put


def self_forward(inputs, self_in, self_out, bias, params, kept):
    projected, shares, context, normed, scale = kept
    for i in range(3):
        projected[:, 512 * i : 512 * i + 512] = dot(inputs[...], self_in[:, 512 * i : 512 * i + 512]).astype(BF16)
    attend(columns_of(projected, 0), columns_of(projected, 512), columns_of(projected, 1024), bias, shares, context)
    branch = dot(context[...], self_out[...])
    return norm(inputs[...].astype(F32) + branch, params, 0, normed, scale)


def self_backward(gradient, inputs, self_in, self_out, kept, grad_context, grad_projected, packed):
    projected, shares, context, normed, scale = kept
    low = gradient.astype(BF16)
    pack(packed, SELF_OUT, dot_tn(context[...], low))
    grad_context[...] = dot_nt(low, self_out[...]).astype(BF16)
    attend_back(columns_of(projected, 0), columns_of(projected, 512), columns_of(projected, 1024), shares, context, grad_context,
                putter(grad_projected, 0), putter(grad_projected, 512), putter(grad_projected, 1024))
    for i in range(3):
        pack(packed, SELF_IN + 2 * i, dot_tn(inputs[...], grad_projected[:, 512 * i : 512 * i + 512]))
    return dot_nt(grad_projected[...], self_in[...])


def ffn_forward(low, hidden_in, hidden_out, activated, slopes):
    for i in range(4):
        hidden = dot(low[...], hidden_in[:, 512 * i : 512 * i + 512])
        cdf = 0.5 * (1.0 + lax.erf(hidden * root_half))
        activated[:, 512 * i : 512 * i + 512] = (hidden * cdf).astype(BF16)
        slopes[:, 512 * i : 512 * i + 512] = cdf + hidden * jnp.exp(-0.5 * hidden * hidden) * inverse_root
    return dot(activated[...], hidden_out[...])


def ffn_backward(gradient, low, hidden_in, hidden_out, activated, slopes, grad_hidden, packed):
    result = gradient.astype(BF16)
    for i in range(4):
        rows = slice(512 * i, 512 * i + 512)
        grad_hidden[:, rows] = (dot_nt(result, hidden_out[rows, :]) * slopes[:, rows]).astype(BF16)
        pack_tall(packed, HIDDEN_OUT, 16 * i, dot_tn(activated[:, rows], result))
    for i in range(4):
        pack(packed, HIDDEN_IN + 2 * i, dot_tn(low[...], grad_hidden[:, 512 * i : 512 * i + 512]))
    return dot_nt(grad_hidden[...], hidden_in[...])


WEIGHT_SHAPES = ((512, 1536), (512, 512), (512, 1024), (512, 2048), (2048, 512))


def keep_attention():
    return [pltpu.VMEM((256, 1536), BF16), pltpu.VMEM((8, 256, 256), BF16), pltpu.VMEM((256, 512), BF16)]


def keep_norm():
    return [pltpu.VMEM((256, 512), F32), pltpu.VMEM((256, 1), F32)]


def keep_ffn():
    return [pltpu.VMEM((256, 512), BF16), pltpu.VMEM((256, 2048), BF16), pltpu.VMEM((256, 2048), F32)]


def pair_kernel(stages, section, lengths, segments, source, target, cot_memory, cot_third, norm_enc, norm_dec, *rest):
    own, other = rest[:5], rest[5:10]
    memory_out, third_out, source_grad, target_grad, packed_enc, packed_dec = rest[10:16]
    rest = list(rest[16:])

    def take(n):
        taken = rest[:n]
        del rest[:n]
        return taken

    enc_w, dec_w = take(5), take(5)
    enc_self = take(5)
    enc_ffn, enc_n1, enc_n2, memory_low, key_value, grad_key_value = take(3), take(2), take(2), *take(3)
    dec_self = take(5)
    queries, cross_shares, cross_context, dec_n2 = *take(3), take(2)
    first_low = take(1)[0]
    dec_ffn, dec_n1 = take(3), take(2)
    bias, cross_bias, target_bias = take(3)
    carry, grad_context, grad_projected, grad_hidden, grad_norms = take(5)
    sems = take(1)[0]

    me = section[0]

    @pl.when(me == 0)
    def _():
        for i in range(5):
            pltpu.make_async_copy(own[i], enc_w[i], sems.at[0, i]).start()
            pltpu.make_async_copy(other[i], dec_w[i], sems.at[1, i]).start()

    @pl.when(me != 0)
    def _():
        for i in range(5):
            pltpu.make_async_copy(other[i], enc_w[i], sems.at[0, i]).start()
            pltpu.make_async_copy(own[i], dec_w[i], sems.at[1, i]).start()

    def ready(j, i):
        pltpu.make_async_copy(own[i], (enc_w, dec_w)[j][i], sems.at[j, i]).wait()

    def stage_masks():
        lane = lax.broadcasted_iota(jnp.int32, (1, ROW), 1)
        down = lax.broadcasted_iota(jnp.int32, (ROW, 1), 0)
        ids_row, ids_col = jnp.zeros((1, ROW), jnp.int32), jnp.zeros((ROW, 1), jnp.int32)
        bound = jnp.int32(0)
        for j in range(NSEG):
            bound = bound + lengths[j]
            ids_row = ids_row + (lane >= bound).astype(jnp.int32)
            ids_col = ids_col + (down >= bound).astype(jnp.int32)
        tgt_row = segments[...].astype(F32)
        tgt_col = jnp.broadcast_to(tgt_row, (128, ROW)).T[:, 0:1]
        ids_row, ids_col = ids_row.astype(F32), ids_col.astype(F32)
        bias[...] = jnp.where(ids_col == ids_row, 0.0, -1e30)
        target_bias[...] = jnp.where(tgt_col == tgt_row, 0.0, -1e30)
        cross_bias[...] = jnp.where(tgt_col == ids_row, 0.0, -1e30)

    def stage_enc_self():
        ready(0, 0)
        ready(0, 1)
        first = self_forward(source, enc_w[0], enc_w[1], bias, norm_enc, enc_self)
        carry[...] = first
        enc_ffn[0][...] = first.astype(BF16)

    def stage_enc_ffn():
        ready(0, 3)
        ready(0, 4)
        result = ffn_forward(enc_ffn[0], enc_w[3], enc_w[4], enc_ffn[1], enc_ffn[2])
        second = norm(carry[...] + result, norm_enc, 1, *enc_n1)
        memory = norm(second, norm_enc, 2, *enc_n2)
        memory_low[...] = memory.astype(BF16)
        memory_out[...] = memory.astype(BF16)
        ready(0, 2)
        for i in range(2):
            key_value[:, 512 * i : 512 * i + 512] = dot(memory_low[...], enc_w[2][:, 512 * i : 512 * i + 512]).astype(BF16)

    def stage_dec_self():
        ready(1, 0)
        ready(1, 1)
        first = self_forward(target, dec_w[0], dec_w[1], target_bias, norm_dec, dec_self)
        carry[...] = first
        first_low[...] = first.astype(BF16)
        ready(1, 2)
        queries[...] = dot(first_low[...], dec_w[2][:, :512]).astype(BF16)

    def stage_dec_cross():
        attend(columns_of(queries, 0), columns_of(key_value, 0), columns_of(key_value, 512), cross_bias, cross_shares, cross_context)
        second = norm(carry[...] + dot(cross_context[...], dec_w[2][:, 512:]), norm_dec, 2, *dec_n2)
        carry[...] = second
        dec_ffn[0][...] = second.astype(BF16)

    def stage_dec_ffn():
        ready(1, 3)
        ready(1, 4)
        third = norm(carry[...] + ffn_forward(dec_ffn[0], dec_w[3], dec_w[4], dec_ffn[1], dec_ffn[2]), norm_dec, 1, *dec_n1)
        third_out[...] = third.astype(BF16)

    def stage_dec_ffn_back():
        gradient = norm_back(cot_third[...].astype(F32), norm_dec, 1, *dec_n1, grad_norms)
        gradient = gradient + ffn_backward(gradient, *dec_ffn[:1], dec_w[3], dec_w[4], *dec_ffn[1:], grad_hidden, packed_dec)
        carry[...] = norm_back(gradient, norm_dec, 2, *dec_n2, grad_norms)

    def stage_dec_cross_back():
        gradient = carry[...]
        low = gradient.astype(BF16)
        pack(packed_dec, CROSS + 2, dot_tn(cross_context[...], low))
        grad_context[...] = dot_nt(low, dec_w[2][:, 512:]).astype(BF16)
        attend_back(columns_of(queries, 0), columns_of(key_value, 0), columns_of(key_value, 512), cross_shares, cross_context, grad_context,
                    putter(grad_projected, 0), putter(grad_key_value, 0), putter(grad_key_value, 512))
        grad_query = grad_projected[:, :512]
        pack(packed_dec, CROSS, dot_tn(first_low[...], grad_query))
        gradient = gradient + dot_nt(grad_query, dec_w[2][:, :512])
        carry[...] = norm_back(gradient, norm_dec, 0, *dec_self[3:], grad_norms)

    def stage_dec_self_back():
        gradient = carry[...]
        target_grad[...] = gradient + self_backward(gradient, target, dec_w[0], dec_w[1], dec_self, grad_context, grad_projected, packed_dec)
        pack_norms(packed_dec, grad_norms)

    def stage_enc_memory_back():
        for i in range(2):
            pack(packed_enc, CROSS + 2 * i, dot_tn(memory_low[...], grad_key_value[:, 512 * i : 512 * i + 512]))
        gradient = cot_memory[...].astype(F32) + dot_nt(grad_key_value[...], enc_w[2][...])
        gradient = norm_back(gradient, norm_enc, 2, *enc_n2, grad_norms)
        carry[...] = norm_back(gradient, norm_enc, 1, *enc_n1, grad_norms)

    def stage_enc_ffn_back():
        gradient = carry[...]
        gradient = gradient + ffn_backward(gradient, enc_ffn[0], enc_w[3], enc_w[4], *enc_ffn[1:], grad_hidden, packed_enc)
        carry[...] = norm_back(gradient, norm_enc, 0, *enc_self[3:], grad_norms)

    def stage_enc_self_back():
        gradient = carry[...]
        source_grad[...] = gradient + self_backward(gradient, source, enc_w[0], enc_w[1], enc_self, grad_context, grad_projected, packed_enc)
        pack_norms(packed_enc, grad_norms)

    steps = [stage_masks, stage_enc_self, stage_enc_ffn, stage_dec_self, stage_dec_cross, stage_dec_ffn, stage_dec_ffn_back,
             stage_dec_cross_back, stage_dec_self_back, stage_enc_memory_back, stage_enc_ffn_back, stage_enc_self_back]
    grad_norms[...] = jnp.zeros_like(grad_norms)
    for step in steps[:stages]:
        step()
    waited = {(0, 0): 2, (0, 1): 2, (0, 3): 3, (0, 4): 3, (0, 2): 3, (1, 0): 4, (1, 1): 4, (1, 2): 4, (1, 3): 6, (1, 4): 6}
    for (j, i), stage in waited.items():
        if stages < stage:
            ready(j, i)


def run_pair(section, lengths, segments, source, target, cot_memory, cot_third, norm_enc, norm_dec, own, other, stages=12, name="pair"):
    weights = [pltpu.VMEM(shape, BF16) for shape in WEIGHT_SHAPES]
    wide = pltpu.VMEM((256, 512), F32)
    low = pltpu.VMEM((256, 512), BF16)
    square = pltpu.VMEM((256, 256), F32)
    scratch = (weights + weights + keep_attention() + keep_norm() + keep_ffn() + keep_norm() + keep_norm()
               + [low, pltpu.VMEM((256, 1024), BF16), pltpu.VMEM((256, 1024), BF16)]
               + keep_attention() + keep_norm() + [low, pltpu.VMEM((8, 256, 256), BF16), low] + keep_norm() + [low] + keep_ffn() + keep_norm()
               + [square] * 3 + [wide, low, pltpu.VMEM((256, 1536), BF16), pltpu.VMEM((256, 2048), BF16), pltpu.VMEM((8, 512), F32)]
               + [pltpu.SemaphoreType.DMA((2, 5))])
    vmem = pl.BlockSpec(memory_space=pltpu.VMEM)
    smem = pl.BlockSpec(memory_space=pltpu.SMEM)
    hbm = pl.BlockSpec(memory_space=pl.ANY)
    packed = jax.ShapeDtypeStruct((64, ROWS_OUT, 128), BF16)
    return pl.pallas_call(
        functools.partial(pair_kernel, stages),
        out_shape=[jax.ShapeDtypeStruct((256, 512), BF16)] * 2 + [jax.ShapeDtypeStruct((256, 512), F32)] * 2 + [packed, packed],
        in_specs=[smem, smem] + [vmem] * 7 + [hbm] * 10,
        out_specs=[vmem] * 6,
        scratch_shapes=scratch,
        compiler_params=pltpu.CompilerParams(vmem_limit_bytes=60 << 20),
        name=name,
    )(section, lengths, segments, source, target, cot_memory, cot_third, norm_enc, norm_dec, *own, *other)


MESH = pl.DeviceIdType.MESH
PARTS = ((0, 160, (0, 1, 2)), (160, 160, (1, 2, 0)), (320, 144, (2, 0, 1)))


def half_of(rows):
    return (rows // 32) * 16


def place():
    dp = lax.axis_index("dp")
    return [lax.div(dp, 16), lax.rem(lax.div(dp, 4), 4), lax.rem(dp, 4)]


def beside(position, axis, step):
    moved = list(position)
    moved[axis] = lax.rem(moved[axis] + (step + 4), 4)
    return {"dp": (moved[0] * 4 + moved[1]) * 4 + moved[2]}


def greet(position):
    barrier = pltpu.get_barrier_semaphore()
    for axis in range(3):
        for step in (1, -1):
            pl.semaphore_signal(barrier, inc=1, device_id=beside(position, axis, step), device_id_type=MESH)
    pl.semaphore_wait(barrier, 6)


def widened(value):
    return value.astype(jnp.float32)


class Ring:
    def __init__(self, source, dim, first, rows, position, axis, scratch, sems):
        self.source, self.dim, self.first, self.rows = source, dim, first, rows
        self.half = half_of(rows)
        self.position, self.axis = position, axis
        self.last, self.next, self.far_last, self.far_next, self.send_last, self.send_next = scratch
        self.sems = sems

    def block(self, step, low, count):
        where = lax.rem(self.position[self.axis] + (step + 4), 4)
        index = [slice(None)] * self.dim + [where]
        index += [slice(None)] * (len(self.source.shape) - 2 - len(index))
        return self.source.at[tuple(index + [pl.ds(self.first + low, count), slice(None)])]

    def copy(self, slot, source, target, step):
        return pltpu.make_async_remote_copy(
            src_ref=source, dst_ref=target, send_sem=self.sems.at[0, slot], recv_sem=self.sems.at[1, slot],
            device_id=beside(self.position, self.axis, step), device_id_type=MESH)

    def rows_of(self, ref, low, count):
        lead = [slice(None)] * (len(ref.shape) - 2)
        return ref.at[tuple(lead + [pl.ds(low, count), slice(None)])]

    def begin(self):
        h, r = self.half, self.rows
        self.copies = [
            self.copy(0, self.block(2, 0, h), self.far_last, 1),
            self.copy(1, self.block(2, h, r - h), self.far_next, -1),
            self.copy(2, self.block(1, h, r - h), self.rows_of(self.last, h, r - h), 1),
            self.copy(3, self.block(-1, 0, h), self.rows_of(self.next, 0, h), -1),
            self.copy(4, self.send_next, self.rows_of(self.last, 0, h), 1),
            self.copy(5, self.send_last, self.rows_of(self.next, h, r - h), -1),
        ]
        for copy in self.copies[:4]:
            copy.start()

    def middle(self):
        h, r = self.half, self.rows
        self.copies[0].wait_recv()
        self.send_next[...] = (widened(self.block(1, 0, h)[...]) + widened(self.far_last[...])).astype(jnp.bfloat16)
        self.copies[4].start()
        self.copies[1].wait_recv()
        self.send_last[...] = (widened(self.block(-1, h, r - h)[...]) + widened(self.far_next[...])).astype(jnp.bfloat16)
        self.copies[5].start()

    def end(self):
        for copy in self.copies[2:]:
            copy.wait_recv()
        return widened(self.block(0, 0, self.rows)[...]) + widened(self.last[...]) + widened(self.next[...])

    def close(self):
        for copy in self.copies:
            copy.wait_send()


def scratch_of(lead, rows):
    h = half_of(rows)
    return [pltpu.VMEM(lead + (n, 128), jnp.bfloat16) for n in (rows, rows, h, rows - h, rows - h, h)]


def sum_kernel(partial_ref, total_ref, *scratch):
    position = place()
    sems = scratch[-1]
    buffers = scratch[:-1]
    greet(position)
    rings = []
    at = 0
    for part, (first, rows, order) in enumerate(PARTS):
        mine = []
        for phase in range(3):
            size = 6 + (1 if phase else 0)
            mine.append(buffers[at : at + size])
            at += size
        rings.append(mine)
    active = []
    for part, (first, rows, order) in enumerate(PARTS):
        active.append(Ring(partial_ref, order[0], first, rows, position, order[0], rings[part][0], sems.at[part, 0]))
    done = []
    for phase in range(3):
        for ring in active:
            ring.begin()
        for ring in active:
            ring.middle()
        following = []
        for part, (first, rows, order) in enumerate(PARTS):
            value = active[part].end()
            done.append(active[part])
            if phase == 2:
                total_ref[first : first + rows, :] = value
                continue
            held = rings[part][phase + 1][6]
            held[...] = value.astype(jnp.bfloat16)
            left = [a for a in (0, 1, 2) if a not in order[: phase + 1]]
            axis = order[phase + 1]
            following.append(Ring(held, left.index(axis), 0, rows, position, axis, rings[part][phase + 1][:6], sems.at[part, phase + 1]))
        active = following
    for ring in done:
        ring.close()


def sum_over_dp(partial):
    shapes = []
    for first, rows, order in PARTS:
        for phase in range(3):
            shapes += scratch_of((4,) * (2 - phase), rows)
            if phase:
                shapes.append(pltpu.VMEM((4,) * (3 - phase) + (rows, 128), jnp.bfloat16))
    return pl.pallas_call(
        sum_kernel,
        out_shape=jax.ShapeDtypeStruct((ROWS_OUT, 128), jnp.float32),
        in_specs=[pl.BlockSpec(memory_space=pltpu.VMEM)],
        out_specs=pl.BlockSpec(memory_space=pltpu.VMEM),
        scratch_shapes=shapes + [pltpu.SemaphoreType.DMA((3, 3, 2, 6))],
        compiler_params=pltpu.CompilerParams(collective_id=1, has_side_effects=True, vmem_limit_bytes=40 << 20),
        name="sum_over_dp",
    )(partial)


def to_partner(value):
    return lax.ppermute(value, "section", [(0, 1), (1, 0)])


def body(tokens, cotangent, source_lengths, target_segments, self_in, self_out, cross_weight, hidden_in, hidden_out, norm_params):
    section = lax.axis_index("section")
    first = section == 0
    own = (self_in[0], self_out[0], cross_weight[0], hidden_in[0], hidden_out[0])
    other = tuple(to_partner(w) for w in own)
    other_norm = to_partner(norm_params[0])
    norm_enc, norm_dec = jnp.where(first, norm_params[0], other_norm), jnp.where(first, other_norm, norm_params[0])

    def both(array):
        held = lax.dynamic_index_in_dim(array[0, :, 0], section, 0, False)
        received = to_partner(lax.dynamic_index_in_dim(array[0, :, 0], 1 - section, 0, False))
        return jnp.where(first, held, received), jnp.where(first, received, held)

    source, target = both(tokens)
    cot_memory, cot_third = both(cotangent)
    lengths = lax.dynamic_index_in_dim(source_lengths[:, 0], section, 0, False)
    segments = lax.dynamic_index_in_dim(target_segments, section, 0, False)
    memory, third, source_grad, target_grad, packed_enc, packed_dec = run_pair(
        section.reshape(1), lengths, segments, source, target, cot_memory, cot_third, norm_enc, norm_dec, own, other)

    def split(enc, dec):
        held, sent = jnp.where(first, enc, dec), jnp.where(first, dec, enc)
        return held, to_partner(sent)

    def joined(enc, dec):
        held, received = split(enc, dec)
        return jnp.where(first, jnp.stack([held, received]), jnp.stack([received, held]))[None, :, None]

    layer_out = joined(memory, third)
    token_grads = joined(source_grad, target_grad)
    held, received = split(packed_enc, packed_dec)
    packed = (held.astype(F32) + received.astype(F32)).astype(BF16)
    total = sum_over_dp(packed.reshape(4, 4, 4, ROWS_OUT, 128))
    results = []
    at = 0
    for w in own:
        rows, columns = w.shape
        count = rows // 64 * columns // 128
        block = total[at : at + count]
        at += count
        if rows == 2048:
            block = block.reshape(4, columns // 128, 8, 128).transpose(0, 2, 1, 3)
        else:
            block = block.reshape(columns // 128, 8, 128).transpose(1, 0, 2)
        results.append(block.reshape(1, rows // 64, columns))
    results.append(total[at : at + 8, :6].T[None])
    return (layer_out, token_grads, *results)


def solution(mesh):
    return jax.shard_map(
        body,
        mesh=mesh,
        in_specs=(
            P("section", None, "dp", None, None),
            P("section", None, "dp", None, None),
            P(None, "dp", None),
            P(None, "dp", None),
            P("section", None, None),
            P("section", None, None),
            P("section", None, None),
            P("section", None, None),
            P("section", None, None),
            P("section", None, None),
        ),
        out_specs=(
            P("section", None, "dp", None, None),
            P("section", None, "dp", None, None),
            P("section", "dp", None),
            P("section", "dp", None),
            P("section", "dp", None),
            P("section", "dp", None),
            P("section", "dp", None),
            P("section", None, "dp"),
        ),
        check_vma=False,
    )
```

profile of v0, /device:TPU:0, one launch (start us, length us, event | category | flops | bytes accessed | tf_op | source)
XLA Modules:
  0.0 132.7 jit_solution(15122901515980458527)
XLA Ops:
  0.7 0.5 collective-permute-start.7
  1.3 1.0 dynamic-slice_bitcast_fusion
  2.3 0.5 collective-permute-start.1
  2.8 0.7 copy.28
  3.6 4.1 %collective-permute-done.2 = f32[6,512]{1,0:T(8,128)S(1)} collective-permute-done((f32[6,512]{1,0:T(8,128)S(1)}, f32[6,512]{1,0:T(8,128)S(1)}, u32[]{:S(2)}, u32[]{:S(2)}) %collective-permute-start.2) | collective-permute-done | bytes 12320 | tf_op jit(solution)/shard_map/ppermute | solution.py:507
  7.9 1.7 %dynamic-slice_bitcast_fusion.1 = bf16[256,512]{1,0:T(8,128)(2,1)} fusion(bf16[1,2,1,256,512]{4,3,2,1,0:T(8,128)(2,1)} %param.10, s32[]{:T(128)S(6)} %select_n.106), kind=kLoop, calls=%fused_computation.11 | loop fusion | bytes 524292 | tf_op jit(solution)/shard_map/jit(dynamic_index_in_dim)/squeeze | solution.py:520
  9.5 0.4 collective-permute-start
  9.9 1.2 fusion.1.lengths
  11.1 0.6 fusion.segments
  11.6 1.1 collective-permute-done
  12.9 1.3 broadcast_select_fusion.3
  14.2 1.8 %bitcast_select_fusion = (bf16[256,512]{1,0:T(8,128)(2,1)}, bf16[256,512]{1,0:T(8,128)(2,1)}) fusion(bf16[256,512]{1,0:T(8,128)(2,1)S(1)} %collective-permute-done.1, pred[]{:T(512)S(6)} %eq.3, bf16[1,2,1,256,512]{4,3,2,1,0:T(8,128)(2,1)} %param.11, s32[]{:T(128)S(6)} %select_n.105), kind=kLoop, calls=%fused_computation.5 | loop fusion | flops 262144 | bytes 1048581 | tf_op jit(solution)/shard_map/jit(_where)/select_n | solution.py:521
  16.0 1.9 %bitcast_select_fusion.2 = (bf16[256,512]{1,0:T(8,128)(2,1)}, bf16[256,512]{1,0:T(8,128)(2,1)}) fusion(bf16[256,512]{1,0:T(8,128)(2,1)} %collective-permute-done, pred[]{:T(512)S(6)} %eq.3, bf16[1,2,1,256,512]{4,3,2,1,0:T(8,128)(2,1)} %param.10, s32[]{:T(128)S(6)} %select_n.105), kind=kLoop, calls=%fused_computation.7 | loop fusion | flops 262144 | bytes 1048581 | tf_op jit(solution)/shard_map/jit(_where)/select_n | solution.py:521
  17.9 0.7 copy-done.3
  18.7 0.3 copy-done.2
  19.0 0.7 copy-done.1
  19.7 35.7 %pair.1 = (bf16[256,512]{1,0:T(8,128)(2,1)}, bf16[256,512]{1,0:T(8,128)(2,1)}, f32[256,512]{1,0:T(8,128)}, f32[256,512]{1,0:T(8,128)}, bf16[64,464,128]{2,1,0:T(8,128)(2,1)}, /*index=5*/bf16[64,464,128]{2,1,0:T(8,128)(2,1)}) custom-call(s32[1]{0:T(128)} %bitcast.section, s32[8]{0:T(128)} %fusion.1.lengths, s32[1,256]{1,0:T(1,128)} %fusion.segments, ...), custom_call_target="tpu_custom_call" | custom-call | tf_op jit(solution)/shard_map/pair/pallas_call | solution.py:346
  55.4 7.4 %broadcast_select_fusion = bf16[64,464,128]{2,1,0:T(8,128)(2,1)} fusion(bf16[64,464,128]{2,1,0:T(8,128)(2,1)} %get-tuple-element.19, bf16[64,464,128]{2,1,0:T(8,128)(2,1)} %get-tuple-element.18, pred[]{:T(512)S(6)} %eq.3), kind=kLoop, calls=%fused_computation.1 | loop fusion | flops 3801088 | bytes 22806528 | tf_op jit(solution)/shard_map/jit(_where)/select_n | solution.py:531
  62.8 0.4 collective-permute-start.10
  63.3 0.2 collective-permute-start.9
  63.6 0.4 collective-permute-start.8
  64.0 8.0 %collective-permute-done.8 = bf16[256,512]{1,0:T(8,128)(2,1)S(1)} collective-permute-done((bf16[256,512]{1,0:T(8,128)(2,1)S(1)}, bf16[256,512]{1,0:T(8,128)(2,1)S(1)}, u32[]{:S(2)}, u32[]{:S(2)}) %collective-permute-start.8) | collective-permute-done | bytes 262176 | tf_op jit(solution)/shard_map/ppermute | solution.py:507
  72.0 0.9 maximum_select_fusion.1
  72.8 1.1 maximum_select_fusion
  73.9 2.2 %collective-permute-done.10 = bf16[64,464,128]{2,1,0:T(8,128)(2,1)S(1)} collective-permute-done((bf16[64,464,128]{2,1,0:T(8,128)(2,1)}, bf16[64,464,128]{2,1,0:T(8,128)(2,1)S(1)}, u32[]{:S(2)}, u32[]{:S(2)}) %collective-permute-start.10) | collective-permute-done | bytes 7602208 | tf_op jit(solution)/shard_map/ppermute | solution.py:507
  76.2 5.9 %add_convert_fusion = bf16[64,464,128]{2,1,0:T(8,128)(2,1)S(1)} fusion(bf16[64,464,128]{2,1,0:T(8,128)(2,1)S(1)} %collective-permute-done.10, bf16[64,464,128]{2,1,0:T(8,128)(2,1)} %get-tuple-element.18, bf16[64,464,128]{2,1,0:T(8,128)(2,1)} %get-tuple-element.19, pred[]{:T(512)S(6)} %eq.3), kind=kLoop, calls=%fused_computation | loop fusion | flops 19005440 | bytes 30408704 | tf_op jit(solution)/shard_map/convert_element_type | solution.py:541
  82.0 47.5 %sum_over_dp.1 = f32[464,128]{1,0:T(8,128)S(1)} custom-call(bf16[4,4,4,464,128]{4,3,2,1,0:T(8,128)(2,1)S(1)} %bitcast.67), custom_call_target="tpu_custom_call" | custom-call | tf_op jit(solution)/shard_map/sum_over_dp/pallas_call | solution.py:495
  129.5 0.6 slice_bitcast_fusion.3
  130.1 0.6 slice_bitcast_fusion.2
  130.8 0.6 slice_bitcast_fusion.1
  131.4 0.7 fusion.2
  132.0 0.7 copy.19
  (28 shorter events, 0.8 us)
Async XLA Ops:
  0.6 10.4 %copy-start = (s32[2,1,256]{2,1,0:T(1,128)S(1)}, s32[2,1,256]{2,1,0:T(1,128)}, u32[]{:S(2)}) copy-start(s32[2,1,256]{2,1,0:T(1,128)} %param.13) | copy-start | bytes 6148
  0.6 17.3 %collective-permute-start.6 = (bf16[512,2048]{1,0:T(8,128)(2,1)}, bf16[512,2048]{1,0:T(8,128)(2,1)S(1)}, u32[]{:S(2)}, u32[]{:S(2)}) collective-permute-start(bf16[512,2048]{1,0:T(8,128)(2,1)} %bitcast.68), channel_id=1, source_target_pairs={{0,64},{64,0},{1,65},{65,1},{2,66},{66,2},{3,67},{67,3},{4,68},{68... | collective-permute-start | bytes 6291464 | tf_op jit(solution)/shard_map/ppermute | solution.py:507
  0.7 17.2 %collective-permute-start.7 = (bf16[2048,512]{1,0:T(8,128)(2,1)}, bf16[2048,512]{1,0:T(8,128)(2,1)}, u32[]{:S(2)}, u32[]{:S(2)}) collective-permute-start(bf16[2048,512]{1,0:T(8,128)(2,1)} %bitcast.70), channel_id=1, source_target_pairs={{0,64},{64,0},{1,65},{65,1},{2,66},{66,2},{3,67},{67,3},{4,68},{68... | collective-permute-start | bytes 6291464 | tf_op jit(solution)/shard_map/ppermute | solution.py:507
  1.2 16.7 %collective-permute-start.3 = (bf16[512,1536]{1,0:T(8,128)(2,1)}, bf16[512,1536]{1,0:T(8,128)(2,1)}, u32[]{:S(2)}, u32[]{:S(2)}) collective-permute-start(bf16[512,1536]{1,0:T(8,128)(2,1)} %bitcast.72), channel_id=1, source_target_pairs={{0,64},{64,0},{1,65},{65,1},{2,66},{66,2},{3,67},{67,3},{4,68},{68... | collective-permute-start | bytes 4718600 | tf_op jit(solution)/shard_map/ppermute | solution.py:507
  2.3 7.2 %collective-permute-start.1 = (bf16[256,512]{1,0:T(8,128)(2,1)S(1)}, bf16[256,512]{1,0:T(8,128)(2,1)S(1)}, u32[]{:S(2)}, u32[]{:S(2)}) collective-permute-start(bf16[256,512]{1,0:T(8,128)(2,1)S(1)} %dynamic-slice_bitcast_fusion), channel_id=1, source_target_pairs={{0,64},{64,0},{1,65},{65,1},{2,66},{66,2},{3,67},{67,3},{4,68},{68... | collective-permute-start | bytes 786440 | tf_op jit(solution)/shard_map/ppermute | solution.py:507
  3.5 4.2 %collective-permute-start.2 = (f32[6,512]{1,0:T(8,128)S(1)}, f32[6,512]{1,0:T(8,128)S(1)}, u32[]{:S(2)}, u32[]{:S(2)}) collective-permute-start(f32[6,512]{1,0:T(8,128)S(1)} %bitcast.81), channel_id=1, source_target_pairs={{0,64},{64,0},{1,65},{65,1},{2,66},{66,2},{3,67},{67,3},{4,68},{68... | collective-permute-start | bytes 36872 | tf_op jit(solution)/shard_map/ppermute | solution.py:507
  7.7 10.2 %collective-permute-start.5 = (bf16[512,1024]{1,0:T(8,128)(2,1)}, bf16[512,1024]{1,0:T(8,128)(2,1)S(1)}, u32[]{:S(2)}, u32[]{:S(2)}) collective-permute-start(bf16[512,1024]{1,0:T(8,128)(2,1)} %bitcast.74), channel_id=1, source_target_pairs={{0,64},{64,0},{1,65},{65,1},{2,66},{66,2},{3,67},{67,3},{4,68},{68... | collective-permute-start | bytes 3145736 | tf_op jit(solution)/shard_map/ppermute | solution.py:507
  9.5 3.2 %collective-permute-start = (bf16[256,512]{1,0:T(8,128)(2,1)}, bf16[256,512]{1,0:T(8,128)(2,1)}, u32[]{:S(2)}, u32[]{:S(2)}) collective-permute-start(bf16[256,512]{1,0:T(8,128)(2,1)} %dynamic-slice_bitcast_fusion.1), channel_id=1, source_target_pairs={{0,64},{64,0},{1,65},{65,1},{2,66},{66,2},{3,67},{67,3},{4,68},{68... | collective-permute-start | bytes 786440 | tf_op jit(solution)/shard_map/ppermute | solution.py:507
  12.8 5.1 %collective-permute-start.4 = (bf16[512,512]{1,0:T(8,128)(2,1)}, bf16[512,512]{1,0:T(8,128)(2,1)S(1)}, u32[]{:S(2)}, u32[]{:S(2)}) collective-permute-start(bf16[512,512]{1,0:T(8,128)(2,1)} %bitcast.76), channel_id=1, source_target_pairs={{0,64},{64,0},{1,65},{65,1},{2,66},{66,2},{3,67},{67,3},{4,68},{68... | collective-permute-start | bytes 1572872 | tf_op jit(solution)/shard_map/ppermute | solution.py:507
  17.9 0.8 copy-start.3
  17.9 1.1 copy-start.2
  17.9 1.8 %copy-start.1 = (bf16[512,2048]{1,0:T(8,128)(2,1)}, bf16[512,2048]{1,0:T(8,128)(2,1)S(1)}, u32[]{:S(2)}) copy-start(bf16[512,2048]{1,0:T(8,128)(2,1)S(1)} %collective-permute-done.6.rest_8_) | copy-start | bytes 6291460
  55.4 7.8 %copy-start.4 = (f32[256,512]{1,0:T(8,128)S(1)}, f32[256,512]{1,0:T(8,128)}, u32[]{:S(2)}) copy-start(f32[256,512]{1,0:T(8,128)} %get-tuple-element.16) | copy-start | bytes 1572868
  55.4 7.8 %copy-start.5 = (f32[256,512]{1,0:T(8,128)S(1)}, f32[256,512]{1,0:T(8,128)}, u32[]{:S(2)}) copy-start(f32[256,512]{1,0:T(8,128)} %get-tuple-element.17) | copy-start | bytes 1572868
  55.4 8.1 %copy-start.6 = (bf16[256,512]{1,0:T(8,128)(2,1)S(1)}, bf16[256,512]{1,0:T(8,128)(2,1)}, u32[]{:S(2)}) copy-start(bf16[256,512]{1,0:T(8,128)(2,1)} %get-tuple-element.14) | copy-start | bytes 786436
  55.4 8.1 %copy-start.7 = (bf16[256,512]{1,0:T(8,128)(2,1)S(1)}, bf16[256,512]{1,0:T(8,128)(2,1)}, u32[]{:S(2)}) copy-start(bf16[256,512]{1,0:T(8,128)(2,1)} %get-tuple-element.15) | copy-start | bytes 786436
  62.8 13.4 %collective-permute-start.10 = (bf16[64,464,128]{2,1,0:T(8,128)(2,1)}, bf16[64,464,128]{2,1,0:T(8,128)(2,1)S(1)}, u32[]{:S(2)}, u32[]{:S(2)}) collective-permute-start(bf16[64,464,128]{2,1,0:T(8,128)(2,1)} %broadcast_select_fusion), channel_id=1, source_target_pairs={{0,64},{64,0},{1,65},{65,1},{2,66},{66,2},{3,67},{67,3},{4,68},{68... | collective-permute-start | bytes 22806536 | tf_op jit(solution)/shard_map/ppermute | solution.py:507
  63.3 9.5 %collective-permute-start.9 = (f32[256,512]{1,0:T(8,128)S(1)}, f32[256,512]{1,0:T(8,128)S(1)}, u32[]{:S(2)}, u32[]{:S(2)}) collective-permute-start(f32[256,512]{1,0:T(8,128)S(1)} %get-tuple-element.29), channel_id=1, source_target_pairs={{0,64},{64,0},{1,65},{65,1},{2,66},{66,2},{3,67},{67,3},{4,68},{68... | collective-permute-start | bytes 1572872 | tf_op jit(solution)/shard_map/ppermute | solution.py:507
  63.6 8.4 %collective-permute-start.8 = (bf16[256,512]{1,0:T(8,128)(2,1)S(1)}, bf16[256,512]{1,0:T(8,128)(2,1)S(1)}, u32[]{:S(2)}, u32[]{:S(2)}) collective-permute-start(bf16[256,512]{1,0:T(8,128)(2,1)S(1)} %get-tuple-element.35), channel_id=1, source_target_pairs={{0,64},{64,0},{1,65},{65,1},{2,66},{66,2},{3,67},{67,3},{4,68},{68... | collective-permute-start | bytes 786440 | tf_op jit(solution)/shard_map/ppermute | solution.py:507
where the time goes:
time: 133 us
  Pallas kernels  83.1 us (62%)
  other arithmetic  20.3 us (15%)
  waiting for transfers between devices  15.5 us (12%)
  local copies, waits for them, and re-layouts  10.1 us (8%)
  starting transfers between devices  2.95 us (2%)
    pallas_call x1, Pallas kernels, sum_over_dp(): pl.pallas_call(sum_kernel, out_shape=jax.ShapeDtypeStruct((ROWS_OUT, 128)...  47.5 us
    pallas_call x1, Pallas kernels, run_pair(): pl.pallas_call(functools.partial(pair_kernel, stages), out_shape=[jax.Sha...  35.7 us
    ppermute x11, waiting for transfers between devices, to_partner(): return lax.ppermute(value, 'section', [(0, 1), (1, 0)])  15.5 us
    select_n x1, other arithmetic, split(): held, sent = (jnp.where(first, enc, dec), jnp.where(first, dec, enc))  7.37 us
    convert_element_type x1, other arithmetic, body(): packed = (held.astype(F32) + received.astype(F32)).astype(BF16)  5.86 us
    select_n x2, other arithmetic, both(): return (jnp.where(first, held, received), jnp.where(first, received, held))  3.66 us
    unnamed x18, local copies, waits for them, and re-layouts  3.19 us
    ppermute x11, starting transfers between devices, to_partner(): return lax.ppermute(value, 'section', [(0, 1), (1, 0)])  2.95 us
  transfers between devices with their start and end apart: 11, of which 4 were waited for; matrix products, arithmetic and copies ran while one was open for 9% of the time, Pallas kernels for 0%

commit v1 on v0

v1 whole, which is shorter than its diff:
```python
import jax
import jax.numpy as jnp
from jax import lax
from jax.experimental import pallas as pl
from jax.experimental.pallas import tpu as pltpu
from jax.sharding import PartitionSpec as P

HEADS = 8
D = 512
ROW = 256
NSEG = 8
root_half = 0.7071067811865476
inverse_root = 0.3989422804014327
F32 = jnp.float32
BF16 = jnp.bfloat16
MESH = pl.DeviceIdType.MESH
WEIGHTS = ((512, 1536), (512, 512), (512, 1024), (512, 2048), (2048, 512))

HIDDEN_OUT, HIDDEN_IN, CROSS, SELF_OUT, SELF_IN, NORMS = 0, 8, 16, 20, 22, 28
GROUPS = (
    (1, 0, 8, (3, 3, 2), 0),
    (1, 16, 6, (2, 2, 2), 1),
    (0, 0, 10, (3, 3, 4), 0),
    (0, 20, 4, (2, 2, 1), 1),
)
BANKS = ((3, 3, 4), (2, 2, 2))
ORDERS = ((0, 1, 2), (1, 2, 0), (2, 0, 1))
STARTS = (0, 16, 28, 48)
PACKED_UNITS = 58


def unit_of(section, unit):
    if section == 1:
        return 57 if unit == NORMS else unit
    return 52 if unit == NORMS else 28 + unit + (1 if unit >= 24 else 0)


def dot(a, b):
    return lax.dot_general(a, b, (((1,), (0,)), ((), ())), preferred_element_type=F32)


def dot_nt(a, b):
    return lax.dot_general(a, b, (((1,), (1,)), ((), ())), preferred_element_type=F32)


def dot_tn(a, b):
    return lax.dot_general(a, b, (((0,), (0,)), ((), ())), preferred_element_type=F32)

def sides(factor):
    lane = lax.broadcasted_iota(jnp.int32, (1, 128), 1)
    low = jnp.where(lane < 64, factor, 0.0).astype(BF16)
    high = jnp.where(lane < 64, 0.0, factor).astype(BF16)
    return (low, high)


def attend(query, key, value, bias, shares, context):
    scaled, plain = sides(0.125), sides(1.0)
    for pair in range(HEADS // 2):
        q, k, v = query(pair), key(pair), value(pair)
        total = None
        for side in range(2):
            scores = dot_nt(q * scaled[side], k) + bias[...]
            expval = jnp.exp(scores - jnp.max(scores, -1, keepdims=True))
            share = (expval * (1.0 / jnp.sum(expval, -1, keepdims=True))).astype(BF16)
            shares[2 * pair + side] = share
            part = dot(share, v * plain[side])
            total = part if total is None else total + part
        context[:, 128 * pair : 128 * pair + 128] = total.astype(BF16)


def attend_back(query, key, value, shares, context, grad_context, put_query, put_key, put_value):
    scaled, plain = sides(0.125), sides(1.0)
    for pair in range(HEADS // 2):
        q, k, v = query(pair), key(pair), value(pair)
        columns = slice(128 * pair, 128 * pair + 128)
        g = grad_context[:, columns]
        along = g.astype(F32) * context[:, columns].astype(F32)
        grads = [None, None, None]
        for side in range(2):
            share = shares[2 * pair + side]
            mine = g * plain[side]
            delta = jnp.sum(along * plain[side].astype(F32), -1, keepdims=True)
            ds = (share.astype(F32) * (dot_nt(mine, v) - delta)).astype(BF16)
            parts = (dot(ds, k * scaled[side]), dot_tn(ds, q * scaled[side]), dot_tn(share, mine))
            grads = [p if t is None else t + p for t, p in zip(grads, parts)]
        for put, grad in zip((put_query, put_key, put_value), grads):
            put(pair, grad.astype(BF16))


def mean(values):
    return jnp.sum(values, -1, keepdims=True) * (1.0 / D)


def norm(values, params, which, normed, scale):
    center = values - mean(values)
    inverse = lax.rsqrt(mean(center * center) + 1e-05)
    result = center * inverse
    normed[...] = result
    scale[...] = inverse
    return result * params[2 * which : 2 * which + 1, :] + params[2 * which + 1 : 2 * which + 2, :]


def norm_back(gradient, params, which, normed, scale, grad_norms):
    n = normed[...]
    grad_norms[2 * which : 2 * which + 1, :] = jnp.sum(gradient * n, 0, keepdims=True)
    grad_norms[2 * which + 1 : 2 * which + 2, :] = jnp.sum(gradient, 0, keepdims=True)
    scaled = gradient * params[2 * which : 2 * which + 1, :]
    return scale[...] * (scaled - mean(scaled) - n * mean(scaled * n))


def pack(packed, section, unit, value):
    blocks = value.reshape(4, 4, 4, 8, value.shape[1])
    for i in range(value.shape[1] // 256):
        two = jnp.concatenate([blocks[..., 256 * i : 256 * i + 128], blocks[..., 256 * i + 128 : 256 * i + 256]], 3)
        at = 16 * unit_of(section, unit + i)
        packed[:, :, :, at : at + 16, :] = two.astype(BF16)


def pack_tall(packed, section, first, value):
    blocks = value.reshape(4, 4, 4, 8, 512)
    for r in range(4):
        for i in range(2):
            two = jnp.concatenate([blocks[:, :, r, :, 256 * i : 256 * i + 128], blocks[:, :, r, :, 256 * i + 128 : 256 * i + 256]], 2)
            at = 16 * unit_of(section, HIDDEN_OUT + 2 * r + i)
            packed[first, :, :, at : at + 16, :] = two.astype(BF16)


def pack_norms(packed, section, grad_norms):
    turned = jnp.concatenate([grad_norms[...], jnp.zeros((120, 512), F32)], 0).T
    tiles = turned.reshape(4, 4, 4, 8, 128)
    at = 16 * unit_of(section, NORMS)
    packed[:, :, :, at : at + 16, :] = jnp.concatenate([tiles, jnp.zeros_like(tiles)], 3).astype(BF16)

def columns_of(ref, first):
    return lambda pair: ref[:, first + 128 * pair : first + 128 * pair + 128]


def putter(ref, first):
    def put(pair, value):
        ref[:, first + 128 * pair : first + 128 * pair + 128] = value

    return put


def thirds(ref):
    return columns_of(ref, 0), columns_of(ref, 512), columns_of(ref, 1024)


def self_forward(inputs, self_in, self_out, bias, params, projected, shares, context, normed, scale):
    for i in range(3):
        projected[:, 512 * i : 512 * i + 512] = dot(inputs[...], self_in[:, 512 * i : 512 * i + 512]).astype(BF16)
    attend(*thirds(projected), bias, shares, context)
    return norm(inputs[...].astype(F32) + dot(context[...], self_out[...]), params, 0, normed, scale)


def ffn_forward(low, hidden_in, hidden_out, activated, slopes, ready_in, ready_out):
    ready_in()
    for i in range(4):
        hidden = dot(low[...], hidden_in[:, 512 * i : 512 * i + 512])
        cdf = 0.5 * (1.0 + lax.erf(hidden * root_half))
        activated[:, 512 * i : 512 * i + 512] = (hidden * cdf).astype(BF16)
        slope = cdf + hidden * jnp.exp(-0.5 * hidden * hidden) * inverse_root
        slopes[:, 512 * i : 512 * i + 512] = slope.astype(BF16)
    ready_out()
    return dot(activated[...], hidden_out[...])


def place():
    dp = lax.axis_index("dp")
    return [lax.div(dp, 16), lax.rem(lax.div(dp, 4), 4), lax.rem(dp, 4)]


def beside(position, axis, step):
    moved = list(position)
    moved[axis] = lax.rem(moved[axis] + (step + 4), 4)
    return {"dp": (moved[0] * 4 + moved[1]) * 4 + moved[2]}


def partner():
    return {"section": 1 - lax.axis_index("section")}


def remote(source, target, send, receive, device):
    return pltpu.make_async_remote_copy(
        src_ref=source, dst_ref=target, send_sem=send, recv_sem=receive, device_id=device, device_id_type=MESH
    )


def widened(ref):
    return ref[...].astype(F32)


def cut(ref, dim, where, rows):
    index = [slice(None)] * (len(ref.shape) - 2)
    index[dim] = where
    return ref.at[tuple(index + [pl.ds(*rows), slice(None)])]


def halved(ref, side):
    return ref.at[pl.ds(2 * side, 2)]


class Part:
    def __init__(self, position, packed, first, rows, order, buffers, sems):
        self.position, self.packed, self.first, self.rows, self.order = position, packed, first, rows, order
        self.buffers, self.sems = buffers, sems
        self.copies = []

    def where(self, axis, step):
        return lax.rem(self.position[axis] + (step + 4), 4)

    def copy(self, phase, slot, source, target, axis, step):
        made = remote(source, target, self.sems.at[0, phase, slot], self.sems.at[1, phase, slot], beside(self.position, axis, step))
        made.start()
        self.copies.append(made)
        return made

    def block(self, step):
        axis = self.order[0]
        return cut(self.packed, axis, self.where(axis, step), (self.first, self.rows))

    def begin(self):
        axis = self.order[0]
        self.last, self.next, self.far_last, self.far_next, self.send_last, self.send_next = [
            ref.at[:, :, pl.ds(0, self.rows), :] for ref in self.buffers[:6]
        ]
        far = self.block(2)
        self.far = [
            self.copy(0, 0, halved(far, 0), self.far_last, axis, 1),
            self.copy(0, 1, halved(far, 1), self.far_next, axis, -1),
        ]
        self.near = [
            self.copy(0, 2, halved(self.block(1), 1), halved(self.last, 1), axis, 1),
            self.copy(0, 3, halved(self.block(-1), 0), halved(self.next, 0), axis, -1),
        ]

    def middle(self):
        axis = self.order[0]
        self.far[0].wait_recv()
        self.send_next[...] = (widened(halved(self.block(1), 0)) + widened(self.far_last)).astype(BF16)
        self.near.append(self.copy(0, 4, self.send_next, halved(self.last, 0), axis, 1))
        self.far[1].wait_recv()
        self.send_last[...] = (widened(halved(self.block(-1), 1)) + widened(self.far_next)).astype(BF16)
        self.near.append(self.copy(0, 5, self.send_last, halved(self.next, 1), axis, -1))

    def end(self):
        for made in self.near:
            made.wait_recv()
        self.held = self.buffers[6]
        self.held[...] = (widened(self.block(0)) + widened(self.last) + widened(self.next)).astype(BF16)
        for made in self.copies:
            made.wait_send()
        self.copies = []

    def direct(self, phase):
        axis = self.order[phase]
        left = sorted(self.order[phase:])
        dim = left.index(axis)
        slots = self.buffers[4 + 4 * phase - 1 : 4 + 4 * phase + 2]
        self.near = [
            self.copy(phase, i, cut(self.held, dim, self.where(axis, step), (0, self.rows)), slots[i], axis, step)
            for i, step in enumerate((2, 1, -1))
        ]
        self.own = (self.held, dim, axis, slots)

    def arrived(self):
        for made in self.near:
            made.wait_recv()
        held, dim, axis, slots = self.own
        total = widened(cut(held, dim, self.where(axis, 0), (0, self.rows)))
        for slot in slots:
            total = total + widened(slot)
        return total

    def hold(self, value):
        self.held = self.buffers[10]
        self.held[...] = value.astype(BF16)

    def close(self):
        for made in self.copies:
            made.wait_send()


def bank_buffers(units):
    rows = 16 * units
    whole, half = (4, 4, rows, 128), (2, 4, rows, 128)
    return [pltpu.VMEM(shape, BF16) for shape in (whole, whole, half, half, half, half)]


def part_buffers(units):
    rows = 16 * units
    one, two = (rows, 128), (4, rows, 128)
    return [pltpu.VMEM(shape, BF16) for shape in ((4, 4, rows, 128), two, two, two, two, one, one, one)]


class Group:
    def __init__(self, which, position, packed, arrivals, totals, banks, own, sems, credits):
        self.section, self.first, self.half, self.parts, self.bank = GROUPS[which]
        self.again = which >= 2
        self.reused = which < 2
        self.position, self.packed, self.totals = position, packed, totals
        self.me = lax.axis_index("section")
        self.swap_sems, self.part_sems, self.total_sems = sems
        self.swap_credit, self.part_credit = credits
        self.units = sum(self.parts)
        self.arrival = arrivals[self.bank]
        self.offsets = [sum(self.parts[:i]) for i in range(3)]
        self.work = []
        for i in range(3):
            first = 16 * (STARTS[which] + self.offsets[i]) + self.me * (16 * self.units)
            first = pl.multiple_of(first, 16)
            buffers = list(banks[self.bank][i]) + list(own[i])
            self.work.append(Part(position, packed, first, 16 * self.parts[i], ORDERS[i], buffers, self.part_sems.at[i]))
        self.swaps = []
        for i in range(3):
            rows = 16 * self.parts[i]
            first = 16 * (STARTS[which] + self.offsets[i]) + (1 - self.me) * (16 * self.units)
            source = packed.at[:, :, :, pl.ds(pl.multiple_of(first, 16), rows), :]
            target = self.arrival.at[:, :, :, pl.ds(16 * self.offsets[i], rows), :]
            self.swaps.append(remote(source, target, self.swap_sems.at[0, i], self.swap_sems.at[1, i], partner()))

    def steps(self):
        if self.again:
            pl.semaphore_wait(self.swap_credit, 1)
        for swap in self.swaps:
            swap.start()
        yield
        for i, part in enumerate(self.work):
            self.swaps[i].wait_recv()
            mine = self.packed.at[:, :, :, pl.ds(part.first, part.rows), :]
            mine[...] = mine[...] + self.arrival[:, :, :, 16 * self.offsets[i] : 16 * self.offsets[i] + part.rows, :]
            if self.again:
                pl.semaphore_wait(self.part_credit.at[i], 2)
            part.begin()
        if self.reused:
            pl.semaphore_signal(self.swap_credit, inc=1, device_id=partner(), device_id_type=MESH)
        yield
        for part in self.work:
            part.middle()
        yield
        for i, part in enumerate(self.work):
            part.end()
            if self.reused:
                for step in (1, -1):
                    pl.semaphore_signal(self.part_credit.at[i], inc=1, device_id=beside(self.position, part.order[0], step), device_id_type=MESH)
            part.direct(1)
        yield
        for part in self.work:
            part.hold(part.arrived())
            part.direct(2)
        yield
        base = 16 * (self.first + self.me * self.half)
        for i, part in enumerate(self.work):
            total = part.arrived()
            at = pl.multiple_of(base + 16 * self.offsets[i], 16)
            if self.offsets[i] < self.half:
                self.totals[self.section, pl.ds(at, part.rows), :] = total
            else:
                self.totals[self.me, 16 * NORMS : 16 * NORMS + 16, :] = total
        mine = self.totals.at[self.section, pl.ds(pl.multiple_of(base, 16), 16 * self.half), :]
        self.handed = remote(mine, mine, self.total_sems.at[0], self.total_sems.at[1], partner())

        @pl.when(self.me != self.section)
        def _():
            self.handed.start()

        yield

    def close(self):
        for swap in self.swaps:
            swap.wait_send()
        for part in self.work:
            part.close()
        theirs = pl.multiple_of(16 * (self.first + (1 - self.me) * self.half), 16)
        other = self.totals.at[self.section, pl.ds(theirs, 16 * self.half), :]

        @pl.when(self.me != self.section)
        def _():
            self.handed.wait_send()

        @pl.when(self.me == self.section)
        def _():
            remote(other, other, self.total_sems.at[0], self.total_sems.at[1], partner()).wait_recv()


def keep_attention():
    return [pltpu.VMEM((256, 1536), BF16), pltpu.VMEM((8, 256, 256), BF16), pltpu.VMEM((256, 512), BF16)]


def keep_norm():
    return [pltpu.VMEM((256, 512), F32), pltpu.VMEM((256, 1), F32)]


def keep_ffn():
    return [pltpu.VMEM((256, 512), BF16), pltpu.VMEM((256, 2048), BF16), pltpu.VMEM((256, 2048), BF16)]


def stacked(scratch):
    return [pltpu.VMEM((2,) + tuple(s.shape), s.dtype) for s in scratch]


def scratch_shapes():
    low, wide, square = pltpu.VMEM((256, 512), BF16), pltpu.VMEM((256, 512), F32), pltpu.VMEM((256, 256), F32)
    return dict(
        weights=stacked([pltpu.VMEM(shape, BF16) for shape in WEIGHTS]),
        inputs=stacked([low, low, pltpu.VMEM((6, 512), F32)]),
        selfs=stacked(keep_attention() + keep_norm()),
        firsts=stacked([low, wide]),
        enc=keep_ffn()[1:] + keep_norm() + keep_norm() + [low, pltpu.VMEM((256, 1024), BF16)],
        cross=[low, pltpu.VMEM((8, 256, 256), BF16), low] + keep_norm(),
        dec=keep_ffn() + keep_norm(),
        bias=[pltpu.VMEM((2, 256, 256), F32), square],
        work=[wide, low, pltpu.VMEM((8, 512), F32)],
        results=[low, wide, low, wide],
        packed=pltpu.VMEM((4, 4, 4, 16 * PACKED_UNITS, 128), BF16),
        arrivals=[pltpu.VMEM((4, 4, 4, 16 * sum(units), 128), BF16) for units in BANKS],
        banks=[[bank_buffers(units) for units in bank] for bank in BANKS],
        parts=[[part_buffers(units) for units in group[3]] for group in GROUPS],
        totals=pltpu.VMEM((2, 464, 128), F32),
        in_sems=pltpu.SemaphoreType.DMA((2, 8)),
        in_sends=pltpu.SemaphoreType.DMA((8,)),
        out_sems=pltpu.SemaphoreType.DMA((3, 2)),
        swap_sems=pltpu.SemaphoreType.DMA((4, 2, 3)),
        part_sems=pltpu.SemaphoreType.DMA((4, 3, 2, 3, 6)),
        total_sems=pltpu.SemaphoreType.DMA((4, 2)),
        swap_credit=pltpu.SemaphoreType.REGULAR((2,)),
        part_credit=pltpu.SemaphoreType.REGULAR((2, 3)),
    )


def whole_kernel(tree, *refs):
    tokens, cotangent, lengths, segments = refs[:4]
    own = refs[4:9]
    norm_params = refs[9]
    layer_out, token_grads = refs[10:12]
    grad_refs, grad_norms_out = refs[12:17], refs[17]
    s = jax.tree.unflatten(tree, refs[18:])
    me = lax.axis_index("section")
    position = place()

    barrier = pltpu.get_barrier_semaphore()
    pl.semaphore_signal(barrier, inc=1, device_id=partner(), device_id_type=MESH)
    for axis in range(3):
        for step in (1, -1):
            pl.semaphore_signal(barrier, inc=1, device_id=beside(position, axis, step), device_id_type=MESH)

    held = list(s["weights"]) + list(s["inputs"])

    def given(i, micro):
        if i < 5:
            return own[i].at[0]
        if i == 7:
            return norm_params.at[0]
        return (tokens, cotangent)[i - 5].at[0, micro, 0]

    def local(i):
        return pltpu.make_async_copy(given(i, me), held[i].at[me], s["in_sems"].at[me, i])

    def sent(i):
        return remote(given(i, 1 - me), held[i].at[me], s["in_sends"].at[i], s["in_sems"].at[me, i], partner())

    def ready(j, i):
        pltpu.make_async_copy(given(i, 0), held[i].at[j], s["in_sems"].at[j, i]).wait()

    for i in (5, 0, 7, 1, 3, 4, 2, 6):
        local(i).start()

    bias, cross_bias = s["bias"]
    lane = lax.broadcasted_iota(jnp.int32, (1, ROW), 1)
    down = lax.broadcasted_iota(jnp.int32, (ROW, 1), 0)
    ids_row, ids_col = jnp.zeros((1, ROW), jnp.int32), jnp.zeros((ROW, 1), jnp.int32)
    bound = jnp.int32(0)
    for j in range(NSEG):
        bound = bound + lengths[me, 0, j]
        ids_row = ids_row + (lane >= bound).astype(jnp.int32)
        ids_col = ids_col + (down >= bound).astype(jnp.int32)
    target_row = segments[me].astype(F32)
    target_col = jnp.broadcast_to(target_row, (128, ROW)).T[:, 0:1]
    ids_row, ids_col = ids_row.astype(F32), ids_col.astype(F32)
    bias[0] = jnp.where(ids_col == ids_row, 0.0, -1e30)
    bias[1] = jnp.where(target_col == target_row, 0.0, -1e30)
    cross_bias[...] = jnp.where(target_col == ids_row, 0.0, -1e30)

    pl.semaphore_wait(barrier, 7)
    for i in (5, 7, 0, 1):
        sent(i).start()

    @pl.when(me == 0)
    def _():
        for i in (3, 4, 2):
            sent(i).start()

    @pl.when(me != 0)
    def _():
        for i in (2, 3, 4):
            sent(i).start()

    sent(6).start()

    w_self_in, w_self_out, w_cross, w_in, w_out = s["weights"]
    x, cot, norms = s["inputs"]
    first_low, first = s["firsts"]
    work, grad_context, grad_norms = s["work"]
    memory_low, source_grad, third_low, target_grad = s["results"]

    def self_block(i, carry):
        j = lax.rem(me + i, 2)
        for which in (5, 0, 7, 1):
            ready(j, which)
        projected, shares, context, normed, scale = [ref.at[j] for ref in s["selfs"]]
        result = self_forward(x.at[j], w_self_in.at[j], w_self_out.at[j], bias.at[j], norms.at[j], projected, shares, context, normed, scale)
        first[j] = result
        first_low[j] = result.astype(BF16)
        return carry

    lax.fori_loop(0, 2, self_block, 0)

    enc_active, enc_slopes, enc_normed, enc_scale, memory_normed, memory_scale, memory_keep, key_value = s["enc"]
    queries, cross_shares, cross_context, cross_normed, cross_scale = s["cross"]
    dec_low, dec_active, dec_slopes, dec_normed, dec_scale = s["dec"]
    enc_self, dec_self = [ref.at[0] for ref in s["selfs"]], [ref.at[1] for ref in s["selfs"]]
    enc_norms, dec_norms = norms.at[0], norms.at[1]

    result = ffn_forward(first_low.at[0], w_in.at[0], w_out.at[0], enc_active, enc_slopes, lambda: ready(0, 3), lambda: ready(0, 4))
    second = norm(first[0] + result, enc_norms, 1, enc_normed, enc_scale)
    memory = norm(second, enc_norms, 2, memory_normed, memory_scale).astype(BF16)
    memory_low[...] = memory
    ready(0, 2)
    for i in range(2):
        key_value[:, 512 * i : 512 * i + 512] = dot(memory, w_cross[0, :, 512 * i : 512 * i + 512]).astype(BF16)

    ready(1, 2)
    queries[...] = dot(first_low[1], w_cross[1, :, :512]).astype(BF16)
    keys_values = (columns_of(key_value, 0), columns_of(key_value, 512))
    attend(columns_of(queries, 0), *keys_values, cross_bias, cross_shares, cross_context)
    second = norm(first[1] + dot(cross_context[...], w_cross[1, :, 512:]), dec_norms, 2, cross_normed, cross_scale)
    dec_low[...] = second.astype(BF16)
    result = ffn_forward(dec_low, w_in.at[1], w_out.at[1], dec_active, dec_slopes, lambda: ready(1, 3), lambda: ready(1, 4))
    third_low[...] = norm(second + result, dec_norms, 1, dec_normed, dec_scale).astype(BF16)

    def put_out(slot, out, values):
        for j in range(2):
            here = pltpu.make_async_copy(values[j], out.at[0, me, 0], s["out_sems"].at[0, slot])
            there = remote(values[j], out.at[0, me, 0], s["out_sems"].at[1, slot], s["out_sems"].at[2, slot], partner())

            @pl.when(me == j)
            def _():
                here.start()

            @pl.when(me != j)
            def _():
                there.start()

    def out_done(slot, out, values):
        pltpu.make_async_copy(values[0], out.at[0, me, 0], s["out_sems"].at[0, slot]).wait()
        there = remote(values[0], out.at[0, me, 0], s["out_sems"].at[1, slot], s["out_sems"].at[2, slot], partner())
        there.wait_send()
        there.wait_recv()

    put_out(0, layer_out, (memory_low, third_low))

    packed = s["packed"]
    groups = [
        Group(g, position, packed, s["arrivals"], s["totals"], s["banks"], s["parts"][g],
              (s["swap_sems"].at[g], s["part_sems"].at[g], s["total_sems"].at[g]),
              (s["swap_credit"].at[GROUPS[g][4]], s["part_credit"].at[GROUPS[g][4]]))
        for g in range(4)
    ]
    running = [group.steps() for group in groups]

    def pump(*which):
        for g in which:
            next(running[g])

    def ffn_back(gradient, low, section, activated, slopes):
        result = gradient.astype(BF16)
        for i in range(4):
            rows = slice(512 * i, 512 * i + 512)
            slopes[:, rows] = (dot_nt(result, w_out[section, rows, :]) * slopes[:, rows].astype(F32)).astype(BF16)
            pack_tall(packed, section, i, dot_tn(activated[:, rows], result))
        for i in range(4):
            pack(packed, section, HIDDEN_IN + 2 * i, dot_tn(low[...], slopes[:, 512 * i : 512 * i + 512]))
        return dot_nt(slopes[...], w_in[section])

    def self_back_a(gradient, section, kept):
        projected, shares, context, normed, scale = kept
        low = gradient.astype(BF16)
        pack(packed, section, SELF_OUT, dot_tn(context[...], low))
        grad_context[...] = dot_nt(low, w_self_out[section]).astype(BF16)

    def self_back_b(section, kept):
        projected, shares, context, normed, scale = kept
        attend_back(*thirds(projected), shares, context, grad_context, *[putter(projected, 512 * i) for i in range(3)])

    def self_back_c(section, kept):
        projected = kept[0]
        for i in range(3):
            pack(packed, section, SELF_IN + 2 * i, dot_tn(x[section], projected[:, 512 * i : 512 * i + 512]))
        pack_norms(packed, section, grad_norms)

    grad_norms[...] = jnp.zeros_like(grad_norms)
    ready(1, 6)
    gradient = norm_back(cot[1].astype(F32), dec_norms, 1, dec_normed, dec_scale, grad_norms)
    gradient = gradient + ffn_back(gradient, dec_low, 1, dec_active, dec_slopes)
    pump(0)
    gradient = norm_back(gradient, dec_norms, 2, cross_normed, cross_scale, grad_norms)
    work[...] = gradient
    low = gradient.astype(BF16)
    pack(packed, 1, CROSS + 2, dot_tn(cross_context[...], low))
    grad_context[...] = dot_nt(low, w_cross[1, :, 512:]).astype(BF16)
    attend_back(columns_of(queries, 0), *keys_values, cross_shares, cross_context, grad_context,
                putter(queries, 0), putter(key_value, 0), putter(key_value, 512))
    pump(0)
    pack(packed, 1, CROSS, dot_tn(first_low[1], queries[...]))
    gradient = work[...] + dot_nt(queries[...], w_cross[1, :, :512])
    gradient = norm_back(gradient, dec_norms, 0, *dec_self[3:], grad_norms)
    work[...] = gradient
    self_back_a(gradient, 1, dec_self)
    pump(0)
    self_back_b(1, dec_self)
    self_back_c(1, dec_self)
    pump(1, 0)
    target_grad[...] = work[...] + dot_nt(dec_self[0][...], w_self_in[1])

    for i in range(2):
        pack(packed, 0, CROSS + 2 * i, dot_tn(memory_low[...], key_value[:, 512 * i : 512 * i + 512]))
    ready(0, 6)
    gradient = cot[0].astype(F32) + dot_nt(key_value[...], w_cross[0])
    gradient = norm_back(gradient, enc_norms, 2, memory_normed, memory_scale, grad_norms)
    gradient = norm_back(gradient, enc_norms, 1, enc_normed, enc_scale, grad_norms)
    pump(1, 0)
    gradient = gradient + ffn_back(gradient, first_low.at[0], 0, enc_active, enc_slopes)
    pump(2, 1, 0)
    gradient = norm_back(gradient, enc_norms, 0, *enc_self[3:], grad_norms)
    work[...] = gradient
    self_back_a(gradient, 0, enc_self)
    pump(1)
    self_back_b(0, enc_self)
    pump(2, 1)
    self_back_c(0, enc_self)
    pump(3, 1)
    source_grad[...] = work[...] + dot_nt(enc_self[0][...], w_self_in[0])
    put_out(1, token_grads, (source_grad, target_grad))
    pump(2, 3, 2, 3, 2, 3, 2, 3, 3)

    for group in groups:
        group.close()
    totals = s["totals"]

    def tile(t):
        return totals[me, 8 * t : 8 * t + 8, :]

    for which, unit, columns in ((0, SELF_IN, 1536), (1, SELF_OUT, 512), (2, CROSS, 1024), (3, HIDDEN_IN, 2048)):
        for i in range(columns // 128):
            grad_refs[which][0, :, 128 * i : 128 * i + 128] = tile(2 * unit + i)
    for r in range(4):
        for i in range(4):
            grad_refs[4][0, 8 * r : 8 * r + 8, 128 * i : 128 * i + 128] = tile(2 * HIDDEN_OUT + 4 * r + i)
    turned = jnp.concatenate([tile(2 * NORMS), jnp.zeros((120, 128), F32)], 0).T
    grad_norms_out[0] = turned[:6, :8]
    for i in range(8):
        sent(i).wait_send()
    out_done(0, layer_out, (memory_low, third_low))
    out_done(1, token_grads, (source_grad, target_grad))


def body(tokens, cotangent, source_lengths, target_segments, self_in, self_out, cross_weight, hidden_in, hidden_out, norm_params):
    shapes, tree = jax.tree.flatten(scratch_shapes())
    vmem, smem, hbm = [pl.BlockSpec(memory_space=space) for space in (pltpu.VMEM, pltpu.SMEM, pl.ANY)]
    f32 = [(1, 8, 1536), (1, 8, 512), (1, 8, 1024), (1, 8, 2048), (1, 32, 512), (1, 6, 8)]
    return tuple(pl.pallas_call(
        lambda *refs: whole_kernel(tree, *refs),
        out_shape=[jax.ShapeDtypeStruct(tokens.shape, BF16), jax.ShapeDtypeStruct(tokens.shape, F32)]
        + [jax.ShapeDtypeStruct(shape, F32) for shape in f32],
        in_specs=[hbm, hbm, smem, vmem] + [hbm] * 6,
        out_specs=[hbm, hbm] + [vmem] * 6,
        scratch_shapes=shapes,
        compiler_params=pltpu.CompilerParams(collective_id=0, has_side_effects=True, vmem_limit_bytes=64 << 20),
        name="layer_pair",
    )(tokens, cotangent, source_lengths, target_segments, self_in, self_out, cross_weight, hidden_in, hidden_out, norm_params))


def solution(mesh):
    return jax.shard_map(
        body,
        mesh=mesh,
        in_specs=(
            P("section", None, "dp", None, None),
            P("section", None, "dp", None, None),
            P(None, "dp", None),
            P(None, "dp", None),
            P("section", None, None),
            P("section", None, None),
            P("section", None, None),
            P("section", None, None),
            P("section", None, None),
            P("section", None, None),
        ),
        out_specs=(
            P("section", None, "dp", None, None),
            P("section", None, "dp", None, None),
            P("section", "dp", None),
            P("section", "dp", None),
            P("section", "dp", None),
            P("section", "dp", None),
            P("section", "dp", None),
            P("section", None, "dp"),
        ),
        check_vma=False,
    )
```

time: 133 us -> 96.6 us (0.73)
  other arithmetic: 20.3 us -> 0 us
  waiting for transfers between devices: 15.5 us -> 0 us
  starting transfers between devices: 2.95 us -> 0 us
  Pallas kernels: 83.1 us -> 85.8 us
    ppermute x11 -> x0, waiting for transfers between devices: 15.5 us -> none  [to_partner(): return lax.ppermute(value, 'section', [(0, 1), (1, 0)])]
    select_n x6 -> x0, other arithmetic: 14.3 us -> none  [the longest x1 7.37 us: split(): held, sent = (jnp.where(first, enc, dec), jnp.where(first, dec, enc))]
    convert_element_type x1 -> x0, other arithmetic: 5.86 us -> none  [body(): packed = (held.astype(F32) + received.astype(F32)).astype(BF16)]
    unnamed x18, local copies, waits for them, and re-layouts: 3.19 us -> 8.56 us
    squeeze x4 -> x0, local copies, waits for them, and re-layouts: 4.36 us -> none  [the longest x2 2.64 us: both(): lax.dynamic_index_in_dim(array[0, :, 0], 1 - section, 0, False)]
    ppermute x11 -> x0, starting transfers between devices: 2.95 us -> none  [to_partner(): return lax.ppermute(value, 'section', [(0, 1), (1, 0)])]
    pallas_call x2 -> x1, Pallas kernels: 83.1 us -> 85.8 us  [body(): pl.pallas_call(lambda *refs: whole_kernel(tree, *refs), out_shape=[jax.Sh...]
    reshape x3 -> x0, local copies, waits for them, and re-layouts: 1.85 us -> none  [body(): results.append(block.reshape(1, rows // 64, columns))]
  transfers between devices with their start and end apart: 11 -> 0, of which waited for: 4 -> 0; matrix products, arithmetic and copies ran while one was open for 9% -> 0% of each run, Pallas kernels for 0% -> 0%
where the time goes in v1:
time: 96.6 us; the launch traced here: 96.3 us
  Pallas kernels  85.8 us (89%)
  local copies, waits for them, and re-layouts  9.88 us (10%)
    pallas_call x1, Pallas kernels, body(): pl.pallas_call(lambda *refs: whole_kernel(tree, *refs), out_shape=[jax.Sh...  85.8 us
    unnamed x18, local copies, waits for them, and re-layouts  8.56 us

profile of v1, /device:TPU:0, one launch (start us, length us, event | category | flops | bytes accessed | tf_op | source)
XLA Modules:
  0.0 96.3 jit_solution(5728060568053578698)
XLA Ops:
  0.6 1.3 %copy.18.refs_9_ = f32[1,6,512]{2,1,0:T(8,128)} copy(f32[1,6,512]{2,0,1:T(1,128)} %param.19) | data formatting | bytes 24576 | tf_op args[9]
  1.9 85.8 %layer_pair.1 = (bf16[1,2,1,256,512]{4,3,2,1,0:T(8,128)(2,1)}, f32[1,2,1,256,512]{4,3,2,1,0:T(8,128)}, f32[1,8,1536]{2,1,0:T(8,128)}, f32[1,8,512]{2,1,0:T(8,128...) custom-call(bf16[1,2,1,256,512]{4,3,2,1,0:T(8,128)(2,1)} %refs_0_.1, ...), custom_call_target="tpu_custom_call" | custom-call | tf_op jit(solution)/shard_map/layer_pair/pallas_call | solution.py:671
  87.7 0.0 copy-start.2
  87.7 0.0 copy-start.4
  87.7 0.0 copy-start.3
  87.7 0.0 copy-start.1
  87.8 0.0 copy-start
  87.8 1.3 %copy.19 = f32[1,6,8]{2,0,1:T(1,128)} copy(f32[1,6,8]{2,1,0:T(8,128)} %get-tuple-element.15) | data formatting | bytes 384 | tf_op jit(solution)/shard_map/layer_pair/pallas_call | solution.py:671
  89.1 1.9 %copy.27 = bf16[1,2,1,256,512]{4,3,2,1,0:T(8,128)(2,1)} copy(bf16[1,2,1,256,512]{4,3,2,1,0:T(8,128)(2,1)} %get-tuple-element.24) | data formatting | bytes 1048576
  91.0 2.3 %copy.28 = f32[1,2,1,256,512]{4,3,2,1,0:T(8,128)} copy(f32[1,2,1,256,512]{4,3,2,1,0:T(8,128)} %get-tuple-element.25) | data formatting | bytes 2097152
  93.2 0.0 copy-done.2
  93.2 0.6 copy.29
  93.8 0.0 copy-done.4
  93.8 0.6 copy.30
  94.4 0.0 copy-done.3
  94.4 0.6 copy.31
  95.1 0.0 copy-done.1
  95.1 0.6 copy.32
  95.7 0.0 copy-done
  95.7 0.6 copy.33
Async XLA Ops:
  87.7 5.5 %copy-start.2 = (f32[1,8,1536]{2,1,0:T(8,128)S(1)}, f32[1,8,1536]{2,1,0:T(8,128)}, u32[]{:S(2)}) copy-start(f32[1,8,1536]{2,1,0:T(8,128)} %get-tuple-element.26) | copy-start | bytes 147460
  87.7 6.1 %copy-start.4 = (f32[1,8,512]{2,1,0:T(8,128)S(1)}, f32[1,8,512]{2,1,0:T(8,128)}, u32[]{:S(2)}) copy-start(f32[1,8,512]{2,1,0:T(8,128)} %get-tuple-element.27) | copy-start | bytes 49156
  87.7 6.7 %copy-start.3 = (f32[1,8,1024]{2,1,0:T(8,128)S(1)}, f32[1,8,1024]{2,1,0:T(8,128)}, u32[]{:S(2)}) copy-start(f32[1,8,1024]{2,1,0:T(8,128)} %get-tuple-element.28) | copy-start | bytes 98308
  87.7 7.3 %copy-start.1 = (f32[1,8,2048]{2,1,0:T(8,128)S(1)}, f32[1,8,2048]{2,1,0:T(8,128)}, u32[]{:S(2)}) copy-start(f32[1,8,2048]{2,1,0:T(8,128)} %get-tuple-element.29) | copy-start | bytes 196612
  87.8 7.9 %copy-start = (f32[1,32,512]{2,1,0:T(8,128)S(1)}, f32[1,32,512]{2,1,0:T(8,128)}, u32[]{:S(2)}) copy-start(f32[1,32,512]{2,1,0:T(8,128)} %get-tuple-element.30) | copy-start | bytes 196612

commit v2 on v1

v2 whole, which is shorter than its diff:
```python
import jax
import jax.numpy as jnp
from jax import lax
from jax.experimental import pallas as pl
from jax.experimental.pallas import tpu as pltpu
from jax.sharding import PartitionSpec as P

HEADS = 8
D = 512
ROW = 256
NSEG = 8
root_half = 0.7071067811865476
inverse_root = 0.3989422804014327
F32 = jnp.float32
BF16 = jnp.bfloat16
MESH = pl.DeviceIdType.MESH
WEIGHTS = ((512, 1536), (512, 512), (512, 1024), (512, 2048), (2048, 512))

HIDDEN_OUT, HIDDEN_IN, CROSS, SELF_OUT, SELF_IN, NORMS = 0, 8, 16, 20, 22, 28
GROUPS = (
    (1, 0, 8, (3, 3, 2), 0),
    (1, 16, 6, (2, 2, 2), 1),
    (0, 0, 10, (3, 3, 4), 0),
    (0, 20, 4, (2, 2, 1), 1),
)
BANKS = ((3, 3, 4), (2, 2, 2))
ORDERS = ((0, 1, 2), (1, 2, 0), (2, 0, 1))
STARTS = (0, 16, 28, 48)
SCHEDULE = dict(
    dec_in3="0s",
    dec_attend="0b 0a",
    dec_end="0c",
    memory_start="1s",
    enc_in0="0b 0a 0c 1a 1b",
    enc_in3="2s 1c",
    enc_start="0b 0c 0a",
    enc_attend="1c 1b 1a 2a",
    enc_end="2b 2c 3s",
    last="1c 1a 3a 0a 2b 3c 2c 1b 3b 2a 1c 0c 3a 3b 3c 2c 2a 2b 3a 3b 3c 0c 2a 2b 0b 1a 2c 1b 3a 3c 3b 1a 0b 1c 1b 2b 2a 0a 3a 2c 3c 3b",
)
PACKED_UNITS = 58


def unit_of(section, unit):
    if section == 1:
        return 57 if unit == NORMS else unit
    return 52 if unit == NORMS else 28 + unit + (1 if unit >= 24 else 0)


def dot(a, b):
    return lax.dot_general(a, b, (((1,), (0,)), ((), ())), preferred_element_type=F32)


def dot_nt(a, b):
    return lax.dot_general(a, b, (((1,), (1,)), ((), ())), preferred_element_type=F32)


def dot_tn(a, b):
    return lax.dot_general(a, b, (((0,), (0,)), ((), ())), preferred_element_type=F32)

def sides(factor):
    lane = lax.broadcasted_iota(jnp.int32, (1, 128), 1)
    low = jnp.where(lane < 64, factor, 0.0).astype(BF16)
    high = jnp.where(lane < 64, 0.0, factor).astype(BF16)
    return (low, high)


def attend(query, key, value, bias, shares, context):
    scaled, plain = sides(0.125), sides(1.0)
    heads = [(pair, side) for pair in range(HEADS // 2) for side in range(2)]
    scores = [dot_nt(query(pair) * scaled[side], key(pair)) + bias[...] for pair, side in heads]
    expvals = [jnp.exp(score - jnp.max(score, -1, keepdims=True)) for score in scores]
    low = [(expval * (1.0 / jnp.sum(expval, -1, keepdims=True))).astype(BF16) for expval in expvals]
    for head in range(HEADS):
        shares[head] = low[head]
    for pair in range(HEADS // 2):
        parts = [dot(low[2 * pair + side], value(pair) * plain[side]) for side in range(2)]
        context[:, 128 * pair : 128 * pair + 128] = (parts[0] + parts[1]).astype(BF16)


def attend_back(query, key, value, shares, context, grad_context, put_query, put_key, put_value):
    scaled, plain = sides(0.125), sides(1.0)
    heads = [(pair, side) for pair in range(HEADS // 2) for side in range(2)]
    given = [grad_context[:, 128 * pair : 128 * pair + 128] for pair in range(HEADS // 2)]
    along = [given[pair].astype(F32) * context[:, 128 * pair : 128 * pair + 128].astype(F32) for pair in range(HEADS // 2)]
    grad_shares = [dot_nt(given[pair] * plain[side], value(pair)) for pair, side in heads]
    deltas = [jnp.sum(along[pair] * plain[side].astype(F32), -1, keepdims=True) for pair, side in heads]
    low = [(shares[i].astype(F32) * (grad_shares[i] - deltas[i])).astype(BF16) for i in range(HEADS)]
    for pair in range(HEADS // 2):
        q, k, g = query(pair), key(pair), given[pair]
        one, two = low[2 * pair], low[2 * pair + 1]
        grad_query = dot(one, k * scaled[0]) + dot(two, k * scaled[1])
        grad_key = dot_tn(one, q * scaled[0]) + dot_tn(two, q * scaled[1])
        grad_value = dot_tn(shares[2 * pair], g * plain[0]) + dot_tn(shares[2 * pair + 1], g * plain[1])
        put_query(pair, grad_query.astype(BF16))
        put_key(pair, grad_key.astype(BF16))
        put_value(pair, grad_value.astype(BF16))


def mean(values):
    return jnp.sum(values, -1, keepdims=True) * (1.0 / D)


def norm(values, params, which, normed, scale):
    center = values - mean(values)
    inverse = lax.rsqrt(mean(center * center) + 1e-05)
    result = center * inverse
    normed[...] = result
    scale[...] = inverse
    return result * params[2 * which] + params[2 * which + 1]


def norm_back(gradient, params, which, normed, scale, grad_norms):
    n = normed[...]
    grad_norms[2 * which : 2 * which + 1, :] = jnp.sum(gradient * n, 0, keepdims=True)
    grad_norms[2 * which + 1 : 2 * which + 2, :] = jnp.sum(gradient, 0, keepdims=True)
    scaled = gradient * params[2 * which]
    return scale[...] * (scaled - mean(scaled) - n * mean(scaled * n))


def pack(packed, section, unit, value):
    blocks = value.reshape(4, 4, 4, 8, value.shape[1])
    for i in range(value.shape[1] // 256):
        two = jnp.concatenate([blocks[..., 256 * i : 256 * i + 128], blocks[..., 256 * i + 128 : 256 * i + 256]], 3)
        at = 16 * unit_of(section, unit + i)
        packed[:, :, :, at : at + 16, :] = two.astype(BF16)


def pack_tall(packed, section, first, value):
    blocks = value.reshape(4, 4, 4, 8, 512)
    for r in range(4):
        for i in range(2):
            two = jnp.concatenate([blocks[:, :, r, :, 256 * i : 256 * i + 128], blocks[:, :, r, :, 256 * i + 128 : 256 * i + 256]], 2)
            at = 16 * unit_of(section, HIDDEN_OUT + 2 * r + i)
            packed[first, :, :, at : at + 16, :] = two.astype(BF16)


def pack_norms(packed, section, grad_norms):
    turned = jnp.concatenate([grad_norms[...], jnp.zeros((120, 512), F32)], 0).T
    tiles = turned.reshape(4, 4, 4, 8, 128)
    at = 16 * unit_of(section, NORMS)
    packed[:, :, :, at : at + 16, :] = jnp.concatenate([tiles, jnp.zeros_like(tiles)], 3).astype(BF16)

def columns_of(ref, first):
    return lambda pair: ref[:, first + 128 * pair : first + 128 * pair + 128]


def putter(ref, first):
    def put(pair, value):
        ref[:, first + 128 * pair : first + 128 * pair + 128] = value

    return put


def thirds(ref):
    return columns_of(ref, 0), columns_of(ref, 512), columns_of(ref, 1024)


def self_forward(inputs, self_in, self_out, bias, params, projected, shares, context, normed, scale):
    for i in range(3):
        projected[:, 512 * i : 512 * i + 512] = dot(inputs[...], self_in[:, 512 * i : 512 * i + 512]).astype(BF16)
    attend(*thirds(projected), bias, shares, context)
    return norm(inputs[...].astype(F32) + dot(context[...], self_out[...]), params, 0, normed, scale)


def ffn_forward(low, hidden_in, hidden_out, activated, slopes, ready_in, ready_out):
    ready_in()
    for i in range(4):
        hidden = dot(low[...], hidden_in[:, 512 * i : 512 * i + 512])
        cdf = 0.5 * (1.0 + lax.erf(hidden * root_half))
        activated[:, 512 * i : 512 * i + 512] = (hidden * cdf).astype(BF16)
        slope = cdf + hidden * jnp.exp(-0.5 * hidden * hidden) * inverse_root
        slopes[:, 512 * i : 512 * i + 512] = slope.astype(BF16)
    ready_out()
    return dot(activated[...], hidden_out[...])


def place():
    dp = lax.axis_index("dp")
    return [lax.div(dp, 16), lax.rem(lax.div(dp, 4), 4), lax.rem(dp, 4)]


def beside(position, axis, step):
    moved = list(position)
    moved[axis] = lax.rem(moved[axis] + (step + 4), 4)
    return {"dp": (moved[0] * 4 + moved[1]) * 4 + moved[2]}


def across(position, axis, step):
    return dict(beside(position, axis, step), section=1 - lax.axis_index("section"))


def partner():
    return {"section": 1 - lax.axis_index("section")}


def remote(source, target, send, receive, device):
    return pltpu.make_async_remote_copy(
        src_ref=source, dst_ref=target, send_sem=send, recv_sem=receive, device_id=device, device_id_type=MESH
    )


def widened(ref):
    return ref[...].astype(F32)


def cut(ref, dim, where, rows):
    index = [slice(None)] * (len(ref.shape) - 2)
    index[dim] = where
    return ref.at[tuple(index + [pl.ds(*rows), slice(None)])]


def halved(ref, side):
    return ref.at[pl.ds(2 * side, 2)]


class Part:
    def __init__(self, group, which, first, rows, at):
        self.group, self.which, self.first = group, which, first
        self.position, self.order = group.position, ORDERS[which]
        self.rows = (at, rows)

    def where(self, axis, step):
        return lax.rem(self.position[axis] + (step + 4), 4)

    def copy(self, receive, source, target, axis, step):
        remote(source, target, self.group.send_sems.at[self.which], receive, beside(self.position, axis, step)).start()

    def block(self, step):
        axis = self.order[0]
        return cut(self.group.packed, axis, self.where(axis, step), (self.first, self.rows[1]))

    def inbox(self, which, side=None):
        rows = [pl.ds(*self.rows), slice(None)]
        middle = [slice(None) if side is None else pl.ds(2 * side, 2), slice(None)]
        return self.group.inbox.at[tuple([which] + middle + rows)]

    def outbox(self, side):
        return self.group.outbox.at[pl.ds(2 * side, 2), :, pl.ds(*self.rows), :]

    def steps(self):
        group, axis, rows = self.group, self.order[0], pl.ds(*self.rows)
        far_sem, near_sem = group.far_sems.at[self.which], group.near_sems.at[self.which]
        group.add_swapped(self.which)
        far = self.block(2)
        self.copy(far_sem, halved(far, 0), self.inbox(2, 0), axis, 1)
        self.copy(far_sem, halved(far, 1), self.inbox(2, 1), axis, -1)
        self.copy(near_sem, halved(self.block(1), 1), self.inbox(0, 1), axis, 1)
        self.copy(near_sem, halved(self.block(-1), 0), self.inbox(1, 0), axis, -1)
        yield
        landed(self.inbox(2), far_sem)
        for side, step in ((0, 1), (1, -1)):
            box = self.outbox(side)
            box[...] = (widened(halved(self.block(step), side)) + widened(self.inbox(2, side))).astype(BF16)
            self.copy(near_sem, box, self.inbox(0 if step == 1 else 1, side), axis, step)
        yield
        landed(group.inbox.at[pl.ds(0, 2), :, :, rows, :], near_sem)
        total = widened(self.block(0)) + widened(self.inbox(0)) + widened(self.inbox(1))
        group.held[0][:, :, self.rows[0] : self.rows[0] + self.rows[1], :] = total.astype(BF16)
        landed(group.inbox.at[:, :, :, rows, :], group.send_sems.at[self.which])
        group.free(self.which)
        self.direct(1)
        yield
        group.held[1][:, self.rows[0] : self.rows[0] + self.rows[1], :] = self.summed(1).astype(BF16)
        self.direct(2)
        yield
        group.total(self.which, self.summed(2))
        yield

    def direct(self, phase):
        axis = self.order[phase]
        dim = sorted(self.order[phase:]).index(axis)
        held, slots = self.group.held[phase - 1], self.group.slots[phase - 1]
        for i, step in enumerate((2, 1, -1)):
            remote(cut(held, dim, self.where(axis, step), self.rows), cut(slots, 0, i, self.rows), self.group.send_sems.at[2 + phase],
                   self.group.direct_sems.at[phase - 1, self.which], beside(self.position, axis, step)).start()

    def summed(self, phase):
        axis = self.order[phase]
        dim = sorted(self.order[phase:]).index(axis)
        held, slots = self.group.held[phase - 1], self.group.slots[phase - 1]
        whole = slots.at[tuple([slice(None)] * (len(slots.shape) - 2) + [pl.ds(*self.rows), slice(None)])]
        landed(whole, self.group.direct_sems.at[phase - 1, self.which])
        total = widened(cut(held, dim, self.where(axis, 0), self.rows))
        for i in range(3):
            total = total + widened(cut(slots, 0, i, self.rows))
        return total


def landed(ref, semaphore):
    pltpu.make_async_copy(ref, ref, semaphore).wait()


def bank_buffers(units):
    rows = 16 * sum(units)
    return [pltpu.VMEM((3, 4, 4, rows, 128), BF16), pltpu.VMEM((4, 4, rows, 128), BF16)]


def group_buffers(units):
    rows = 16 * sum(units)
    return [pltpu.VMEM(shape + (rows, 128), BF16) for shape in ((4, 4), (4,), (3, 4), (3,))]


class Group:
    def __init__(self, which, position, packed, arrivals, totals, banks, own, sems, credits):
        self.section, self.first, self.half, self.parts, self.bank = GROUPS[which]
        self.again, self.reused = which >= 2, which < 2
        self.position, self.packed, self.totals = position, packed, totals
        self.me = lax.axis_index("section")
        self.swap_sems, self.far_sems, self.near_sems, self.direct_sems, self.send_sems, self.total_sems = sems
        self.swap_credit, self.part_credit = credits
        self.units = sum(self.parts)
        rows = 16 * self.units
        self.arrival = arrivals[self.bank]
        self.inbox, self.outbox = banks[self.bank]
        self.inbox = self.inbox.at[:, :, :, pl.ds(0, rows), :]
        self.held, self.slots = own[:2], own[2:]
        self.offsets = [sum(self.parts[:i]) for i in range(3)]
        self.start, self.other = [
            pl.multiple_of(16 * STARTS[which] + side * rows, 16) for side in (self.me, 1 - self.me)
        ]
        self.work = [Part(self, i, self.start + 16 * self.offsets[i], 16 * self.parts[i], 16 * self.offsets[i]) for i in range(3)]

    def swap(self, i):
        rows = 16 * self.parts[i]
        source = self.packed.at[:, :, :, pl.ds(self.other + 16 * self.offsets[i], rows), :]
        target = self.arrival.at[:, :, :, pl.ds(16 * self.offsets[i], rows), :]
        return remote(source, target, self.swap_sems.at[3], self.swap_sems.at[i], partner())

    def start_swap(self):
        self.begun = self.ended = 0
        if self.again:
            pl.semaphore_wait(self.swap_credit, 1)
        for i in range(3):
            self.swap(i).start()
        self.steps = [part.steps() for part in self.work]

    def add_swapped(self, i):
        part = self.work[i]
        self.swap(i).wait_recv()
        mine = self.packed.at[:, :, :, pl.ds(part.first, part.rows[1]), :]
        mine[...] = mine[...] + self.arrival[:, :, :, part.rows[0] : part.rows[0] + part.rows[1], :]
        self.begun += 1
        if self.reused and self.begun == 3:
            pl.semaphore_signal(self.swap_credit, inc=1, device_id=partner(), device_id_type=MESH)
        if self.again:
            pl.semaphore_wait(self.part_credit.at[i], 2)

    def free(self, i):
        if self.reused:
            for step in (1, -1):
                pl.semaphore_signal(self.part_credit.at[i], inc=1, device_id=beside(self.position, ORDERS[i][0], step), device_id_type=MESH)

    def total(self, i, total):
        base = 16 * (self.first + self.me * self.half)
        if self.offsets[i] < self.half:
            at = pl.multiple_of(base + 16 * self.offsets[i], 16)
            self.totals[self.section, pl.ds(at, 16 * self.parts[i]), :] = total
        else:
            self.totals[self.me, 16 * NORMS : 16 * NORMS + 16, :] = total
        self.ended += 1
        if self.ended < 3:
            return
        mine = self.totals.at[self.section, pl.ds(pl.multiple_of(base, 16), 16 * self.half), :]
        self.handed = remote(mine, mine, self.total_sems.at[0], self.total_sems.at[1], partner())

        @pl.when(self.me != self.section)
        def _():
            self.handed.start()

    def close(self):
        landed(self.packed.at[:, :, :, pl.ds(self.other, 16 * self.units), :], self.swap_sems.at[3])
        landed(self.slots[0], self.send_sems.at[3])
        landed(self.slots[1], self.send_sems.at[4])
        theirs = pl.multiple_of(16 * (self.first + (1 - self.me) * self.half), 16)

        @pl.when(self.me != self.section)
        def _():
            self.handed.wait_send()

        @pl.when(self.me == self.section)
        def _():
            landed(self.totals.at[self.section, pl.ds(theirs, 16 * self.half), :], self.total_sems.at[1])


def keep_attention():
    return [pltpu.VMEM((256, 1536), BF16), pltpu.VMEM((8, 256, 256), BF16), pltpu.VMEM((256, 512), BF16)]


def keep_norm():
    return [pltpu.VMEM((256, 512), F32), pltpu.VMEM((256, 1), F32)]


def keep_ffn():
    return [pltpu.VMEM((256, 512), BF16), pltpu.VMEM((256, 2048), BF16), pltpu.VMEM((256, 2048), BF16)]


def stacked(scratch):
    return [pltpu.VMEM((2,) + tuple(s.shape), s.dtype) for s in scratch]


def scratch_shapes():
    low, wide, square = pltpu.VMEM((256, 512), BF16), pltpu.VMEM((256, 512), F32), pltpu.VMEM((256, 256), F32)
    return dict(
        weights=stacked([pltpu.VMEM(shape, BF16) for shape in WEIGHTS]),
        inputs=stacked([low, low, pltpu.VMEM((6, 1, 512), F32)]),
        selfs=stacked(keep_attention() + keep_norm()),
        firsts=stacked([low, wide]),
        enc=keep_ffn()[1:] + keep_norm() + keep_norm() + [low, pltpu.VMEM((256, 1024), BF16)],
        cross=[low, pltpu.VMEM((8, 256, 256), BF16), low] + keep_norm(),
        dec=keep_ffn() + keep_norm(),
        bias=[pltpu.VMEM((2, 256, 256), F32), square],
        work=[wide, low, pltpu.VMEM((8, 512), F32)],
        results=[low, low],
        packed=pltpu.VMEM((4, 4, 4, 16 * PACKED_UNITS, 128), BF16),
        arrivals=[pltpu.VMEM((4, 4, 4, 16 * sum(units), 128), BF16) for units in BANKS],
        banks=[bank_buffers(units) for units in BANKS],
        groups=[group_buffers(group[3]) for group in GROUPS],
        places=[pltpu.VMEM((2, 1, ROW), jnp.int32), pltpu.SMEM((2, 1, NSEG), jnp.int32)],
        totals=pltpu.VMEM((2, 464, 128), F32),
        in_sems=pltpu.SemaphoreType.DMA((2, 8)),
        in_sends=pltpu.SemaphoreType.DMA((8,)),
        place_sems=pltpu.SemaphoreType.DMA((2,)),
        out_sems=pltpu.SemaphoreType.DMA((3, 2)),
        group_sems=[
            [pltpu.SemaphoreType.DMA(shape) for shape in ((4,), (3,), (3,), (2, 3), (5,), (2,))]
            for _ in GROUPS
        ],
        swap_credit=pltpu.SemaphoreType.REGULAR((2,)),
        part_credit=pltpu.SemaphoreType.REGULAR((2, 3)),
    )


def whole_kernel(tree, *refs):
    tokens, cotangent, lengths_in, segments_in = refs[:4]
    own = refs[4:9]
    norm_params = refs[9]
    layer_out, token_grads = refs[10:12]
    totals_out = refs[12]
    s = jax.tree.unflatten(tree, refs[13:])
    me = lax.axis_index("section")
    position = place()

    barrier = pltpu.get_barrier_semaphore()
    pl.semaphore_signal(barrier, inc=1, device_id=partner(), device_id_type=MESH)
    for axis in range(3):
        for step in (1, -1):
            pl.semaphore_signal(barrier, inc=1, device_id=beside(position, axis, step), device_id_type=MESH)
            pl.semaphore_signal(barrier, inc=1, device_id=across(position, axis, step), device_id_type=MESH)

    held = list(s["weights"]) + list(s["inputs"])

    def given(i, micro):
        if i < 5:
            return own[i].at[0]
        if i == 7:
            return norm_params
        return (tokens, cotangent)[i - 5].at[0, micro, 0]

    def local(i):
        return pltpu.make_async_copy(given(i, me), held[i].at[me], s["in_sems"].at[me, i])

    def sent(i):
        return remote(given(i, 1 - me), held[i].at[me], s["in_sends"].at[i], s["in_sems"].at[me, i], partner())

    def ready(j, i):
        pltpu.make_async_copy(given(i, 0), held[i].at[j], s["in_sems"].at[j, i]).wait()

    segments, lengths = s["places"]
    places = [pltpu.make_async_copy((segments_in, lengths_in)[i], s["places"][i], s["place_sems"].at[i]) for i in range(2)]
    for copy in places:
        copy.start()
    for i in (5, 0, 7, 1, 3, 4, 2, 6):
        local(i).start()
    for copy in places:
        copy.wait()

    bias, cross_bias = s["bias"]
    lane = lax.broadcasted_iota(jnp.int32, (1, ROW), 1)
    down = lax.broadcasted_iota(jnp.int32, (ROW, 1), 0)
    ids_row, ids_col = jnp.zeros((1, ROW), jnp.int32), jnp.zeros((ROW, 1), jnp.int32)
    bound = jnp.int32(0)
    for j in range(NSEG):
        bound = bound + lengths[me, 0, j]
        ids_row = ids_row + (lane >= bound).astype(jnp.int32)
        ids_col = ids_col + (down >= bound).astype(jnp.int32)
    target_row = segments[me].astype(F32)
    target_col = jnp.broadcast_to(target_row, (128, ROW)).T[:, 0:1]
    ids_row, ids_col = ids_row.astype(F32), ids_col.astype(F32)
    bias[0] = jnp.where(ids_col == ids_row, 0.0, -1e30)
    bias[1] = jnp.where(target_col == target_row, 0.0, -1e30)
    cross_bias[...] = jnp.where(target_col == ids_row, 0.0, -1e30)

    pl.semaphore_wait(barrier, 13)
    for i in (5, 7, 0, 1):
        sent(i).start()
    first = 0
    for k, rows in enumerate((352, 352, 336, 336, 336, 336)):
        piece = pl.ds(first, rows)
        remote(own[4].at[0, piece], held[4].at[me, piece], s["in_sends"].at[4], s["in_sems"].at[me, 4],
               across(position, k // 2, 1 - 2 * (k % 2))).start()
        first += rows

    @pl.when(me == 0)
    def _():
        for i in (3, 2):
            sent(i).start()

    @pl.when(me != 0)
    def _():
        for i in (2, 3):
            sent(i).start()

    sent(6).start()

    w_self_in, w_self_out, w_cross, w_in, w_out = s["weights"]
    x, cot, norms = s["inputs"]
    first_low, first = s["firsts"]
    work, grad_context, grad_norms = s["work"]
    memory_low, third_low = s["results"]
    source_grad, target_grad = first.at[0], first.at[1]

    def self_block(i, carry):
        j = lax.rem(me + i, 2)
        for which in (5, 0, 7, 1):
            ready(j, which)
        projected, shares, context, normed, scale = [ref.at[j] for ref in s["selfs"]]
        result = self_forward(x.at[j], w_self_in.at[j], w_self_out.at[j], bias.at[j], norms.at[j], projected, shares, context, normed, scale)
        first[j] = result
        first_low[j] = result.astype(BF16)
        return carry

    lax.fori_loop(0, 2, self_block, 0)

    enc_active, enc_slopes, enc_normed, enc_scale, memory_normed, memory_scale, memory_keep, key_value = s["enc"]
    queries, cross_shares, cross_context, cross_normed, cross_scale = s["cross"]
    dec_low, dec_active, dec_slopes, dec_normed, dec_scale = s["dec"]
    enc_self, dec_self = [ref.at[0] for ref in s["selfs"]], [ref.at[1] for ref in s["selfs"]]
    enc_norms, dec_norms = norms.at[0], norms.at[1]

    result = ffn_forward(first_low.at[0], w_in.at[0], w_out.at[0], enc_active, enc_slopes, lambda: ready(0, 3), lambda: ready(0, 4))
    second = norm(first[0] + result, enc_norms, 1, enc_normed, enc_scale)
    memory = norm(second, enc_norms, 2, memory_normed, memory_scale).astype(BF16)
    memory_low[...] = memory
    ready(0, 2)
    for i in range(2):
        key_value[:, 512 * i : 512 * i + 512] = dot(memory, w_cross[0, :, 512 * i : 512 * i + 512]).astype(BF16)

    ready(1, 2)
    queries[...] = dot(first_low[1], w_cross[1, :, :512]).astype(BF16)
    keys_values = (columns_of(key_value, 0), columns_of(key_value, 512))
    attend(columns_of(queries, 0), *keys_values, cross_bias, cross_shares, cross_context)
    second = norm(first[1] + dot(cross_context[...], w_cross[1, :, 512:]), dec_norms, 2, cross_normed, cross_scale)
    dec_low[...] = second.astype(BF16)
    result = ffn_forward(dec_low, w_in.at[1], w_out.at[1], dec_active, dec_slopes, lambda: ready(1, 3), lambda: ready(1, 4))
    third_low[...] = norm(second + result, dec_norms, 1, dec_normed, dec_scale).astype(BF16)

    def put_out(slot, out, values):
        for j in range(2):
            here = pltpu.make_async_copy(values[j], out.at[0, me, 0], s["out_sems"].at[0, slot])
            there = remote(values[j], out.at[0, me, 0], s["out_sems"].at[1, slot], s["out_sems"].at[2, slot], partner())

            @pl.when(me == j)
            def _():
                here.start()

            @pl.when(me != j)
            def _():
                there.start()

    def out_done(slot, out, values):
        pltpu.make_async_copy(values[0], out.at[0, me, 0], s["out_sems"].at[0, slot]).wait()
        there = remote(values[0], out.at[0, me, 0], s["out_sems"].at[1, slot], s["out_sems"].at[2, slot], partner())
        there.wait_send()
        there.wait_recv()

    put_out(0, layer_out, (memory_low, third_low))

    packed = s["packed"]
    groups = [
        Group(g, position, packed, s["arrivals"], s["totals"], s["banks"], s["groups"][g], s["group_sems"][g],
              (s["swap_credit"].at[GROUPS[g][4]], s["part_credit"].at[GROUPS[g][4]]))
        for g in range(4)
    ]
    def at(moment, which=None):
        for step in SCHEDULE.get(moment if which is None else moment + str(which), "").split():
            group = groups[int(step[0])]
            if step[1] == "s":
                group.start_swap()
            else:
                next(group.steps["abc".index(step[1])])

    def ffn_back(gradient, low, section, activated, slopes, moment):
        result = gradient.astype(BF16)
        for i in range(4):
            rows = slice(512 * i, 512 * i + 512)
            slopes[:, rows] = (dot_nt(result, w_out[section, rows, :]) * slopes[:, rows].astype(F32)).astype(BF16)
            pack_tall(packed, section, i, dot_tn(activated[:, rows], result))
            at(moment + "_out", i)
        for i in range(4):
            pack(packed, section, HIDDEN_IN + 2 * i, dot_tn(low[...], slopes[:, 512 * i : 512 * i + 512]))
            at(moment + "_in", i)
        return dot_nt(slopes[...], w_in[section])

    def self_back_a(gradient, section, kept):
        projected, shares, context, normed, scale = kept
        low = gradient.astype(BF16)
        pack(packed, section, SELF_OUT, dot_tn(context[...], low))
        grad_context[...] = dot_nt(low, w_self_out[section]).astype(BF16)

    def self_back_b(section, kept, moment):
        projected, shares, context, normed, scale = kept
        attend_back(*thirds(projected), shares, context, grad_context, *[putter(projected, 512 * i) for i in range(3)])
        at(moment + "_attend")

    def self_back_c(section, kept):
        projected = kept[0]
        for i in range(3):
            pack(packed, section, SELF_IN + 2 * i, dot_tn(x[section], projected[:, 512 * i : 512 * i + 512]))
        pack_norms(packed, section, grad_norms)

    grad_norms[...] = jnp.zeros_like(grad_norms)
    ready(1, 6)
    gradient = norm_back(cot[1].astype(F32), dec_norms, 1, dec_normed, dec_scale, grad_norms)
    gradient = gradient + ffn_back(gradient, dec_low, 1, dec_active, dec_slopes, "dec")
    gradient = norm_back(gradient, dec_norms, 2, cross_normed, cross_scale, grad_norms)
    work[...] = gradient
    low = gradient.astype(BF16)
    pack(packed, 1, CROSS + 2, dot_tn(cross_context[...], low))
    grad_context[...] = dot_nt(low, w_cross[1, :, 512:]).astype(BF16)
    at("cross_start")
    attend_back(columns_of(queries, 0), *keys_values, cross_shares, cross_context, grad_context,
                putter(queries, 0), putter(key_value, 0), putter(key_value, 512))
    at("cross_attend")
    pack(packed, 1, CROSS, dot_tn(first_low[1], queries[...]))
    gradient = work[...] + dot_nt(queries[...], w_cross[1, :, :512])
    gradient = norm_back(gradient, dec_norms, 0, *dec_self[3:], grad_norms)
    work[...] = gradient
    at("cross_end")
    self_back_a(gradient, 1, dec_self)
    at("dec_start")
    self_back_b(1, dec_self, "dec")
    self_back_c(1, dec_self)
    at("dec_end")
    target_grad[...] = work[...] + dot_nt(dec_self[0][...], w_self_in[1])

    for i in range(2):
        pack(packed, 0, CROSS + 2 * i, dot_tn(memory_low[...], key_value[:, 512 * i : 512 * i + 512]))
    at("memory_start")
    ready(0, 6)
    gradient = cot[0].astype(F32) + dot_nt(key_value[...], w_cross[0])
    gradient = norm_back(gradient, enc_norms, 2, memory_normed, memory_scale, grad_norms)
    gradient = norm_back(gradient, enc_norms, 1, enc_normed, enc_scale, grad_norms)
    at("memory_end")
    gradient = gradient + ffn_back(gradient, first_low.at[0], 0, enc_active, enc_slopes, "enc")
    gradient = norm_back(gradient, enc_norms, 0, *enc_self[3:], grad_norms)
    work[...] = gradient
    self_back_a(gradient, 0, enc_self)
    at("enc_start")
    self_back_b(0, enc_self, "enc")
    self_back_c(0, enc_self)
    at("enc_end")
    source_grad[...] = work[...] + dot_nt(enc_self[0][...], w_self_in[0])
    put_out(1, token_grads, (source_grad, target_grad))
    at("last")

    for group in groups:
        group.close()
    copy = pltpu.make_async_copy(s["totals"].at[me], totals_out, s["place_sems"].at[0])
    copy.start()
    for i in range(8):
        sent(i).wait_send()
    out_done(0, layer_out, (memory_low, third_low))
    out_done(1, token_grads, (source_grad, target_grad))
    copy.wait()


def finish_kernel(layer_in, grads_in, totals, layer_out, token_grads, *refs):
    grad_refs, grad_norms = refs[:5], refs[5]
    layer_out[...] = layer_in[...]
    token_grads[...] = grads_in[...]

    def tile(t):
        return totals[8 * t : 8 * t + 8, :]

    for which, unit, columns in ((0, SELF_IN, 1536), (1, SELF_OUT, 512), (2, CROSS, 1024), (3, HIDDEN_IN, 2048)):
        for i in range(columns // 128):
            grad_refs[which][0, :, 128 * i : 128 * i + 128] = tile(2 * unit + i)
    for r in range(4):
        for i in range(4):
            grad_refs[4][0, 8 * r : 8 * r + 8, 128 * i : 128 * i + 128] = tile(2 * HIDDEN_OUT + 4 * r + i)
    turned = jnp.concatenate([tile(2 * NORMS), jnp.zeros((120, 128), F32)], 0).T
    for i in range(6):
        grad_norms[i] = turned[i : i + 1, :8]


def body(tokens, cotangent, source_lengths, target_segments, self_in, self_out, cross_weight, hidden_in, hidden_out, norm_params):
    shapes, tree = jax.tree.flatten(scratch_shapes())
    vmem, hbm = [pl.BlockSpec(memory_space=space) for space in (pltpu.VMEM, pl.ANY)]
    large = [jax.ShapeDtypeStruct(tokens.shape, BF16), jax.ShapeDtypeStruct(tokens.shape, F32)]
    layer, grads, totals = pl.pallas_call(
        lambda *refs: whole_kernel(tree, *refs),
        out_shape=large + [jax.ShapeDtypeStruct((464, 128), F32)],
        in_specs=[hbm] * 10,
        out_specs=[hbm] * 3,
        scratch_shapes=shapes,
        compiler_params=pltpu.CompilerParams(collective_id=0, has_side_effects=True, vmem_limit_bytes=64 << 20),
        name="layer_pair",
    )(tokens, cotangent, source_lengths, target_segments, self_in, self_out, cross_weight, hidden_in, hidden_out,
      norm_params.transpose(1, 0, 2))
    small = [(1, 8, 1536), (1, 8, 512), (1, 8, 1024), (1, 8, 2048), (1, 32, 512), (6, 1, 8)]
    results = pl.pallas_call(
        finish_kernel,
        out_shape=large + [jax.ShapeDtypeStruct(shape, F32) for shape in small],
        in_specs=[vmem] * 3,
        out_specs=[vmem] * 8,
        name="finish",
    )(layer, grads, totals)
    return (*results[:7], results[7].transpose(1, 0, 2))


def solution(mesh):
    return jax.shard_map(
        body,
        mesh=mesh,
        in_specs=(
            P("section", None, "dp", None, None),
            P("section", None, "dp", None, None),
            P(None, "dp", None),
            P(None, "dp", None),
            P("section", None, None),
            P("section", None, None),
            P("section", None, None),
            P("section", None, None),
            P("section", None, None),
            P("section", None, None),
        ),
        out_specs=(
            P("section", None, "dp", None, None),
            P("section", None, "dp", None, None),
            P("section", "dp", None),
            P("section", "dp", None),
            P("section", "dp", None),
            P("section", "dp", None),
            P("section", "dp", None),
            P("section", None, "dp"),
        ),
        check_vma=False,
    )
```

time: 96.6 us -> 72.4 us (0.75); the launches traced: 96.3 us -> 70.9 us
  Pallas kernels: 85.8 us -> 70.3 us
  local copies, waits for them, and re-layouts: 9.88 us -> 0 us
    pallas_call x1 -> x2, Pallas kernels: 85.8 us -> 70.3 us  [the longest x1 67.6 us: body(): pl.pallas_call(lambda *refs: whole_kernel(tree, *refs), out_shape=large +...]
    unnamed x18 -> x0, local copies, waits for them, and re-layouts: 8.56 us -> none
    pallas_call x1 -> x0, local copies, waits for them, and re-layouts: 1.32 us -> none  [body(): pl.pallas_call(lambda *refs: whole_kernel(tree, *refs), out_shape=[jax.Sh...]
where the time goes in v2:
time: 72.4 us; the launch traced here: 70.9 us
  Pallas kernels  70.3 us (97%)
    pallas_call x1, Pallas kernels, body(): pl.pallas_call(lambda *refs: whole_kernel(tree, *refs), out_shape=large +...  67.6 us
    pallas_call x1, Pallas kernels, body(): pl.pallas_call(finish_kernel, out_shape=large + [jax.ShapeDtypeStruct(sha...  2.69 us

profile of v2, /device:TPU:0, one launch (start us, length us, event | category | flops | bytes accessed | tf_op | source)
XLA Modules:
  0.0 70.9 jit_solution(3961766754002461646)
XLA Ops:
  0.6 67.6 %layer_pair.1 = (bf16[1,2,1,256,512]{4,3,2,1,0:T(8,128)(2,1)}, f32[1,2,1,256,512]{4,3,2,1,0:T(8,128)}, f32[464,128]{1,0:T(8,128)}) custom-call(bf16[1,2,1,256,512]{4,3,2,1,0:T(8,128)(2,1)} %refs_0_.1, bf16[1,2,1,256,512]{4,3,2,1,0:T(8,128)(2,1)} %refs_1_.1, s32[2,1,8]{2,1,0:T(1,128)} %refs_2_.1, s32[2,1,256]{2,1,0:T(1,128)} %refs_3_.1, ...), custom_call_target="tpu_custom_call" | custom-call | tf_op jit(solution)/shard_map/layer_pair/pallas_call | solution.py:701
  68.3 2.7 %finish.1 = (bf16[1,2,1,256,512]{4,3,2,1,0:T(8,128)(2,1)}, f32[1,2,1,256,512]{4,3,2,1,0:T(8,128)}, f32[1,8,1536]{2,1,0:T(8,128)}, f32[1,8,512]{2,1,0:T(8,128)}, ...) custom-call(bf16[1,2,1,256,512]{4,3,2,1,0:T(8,128)(2,1)} %get-tuple-element.19.layer_, ...), custom_call_target="tpu_custom_call" | custom-call | tf_op jit(solution)/shard_map/finish/pallas_call | solution.py:712

commit v3 on v2

--- a/solution.py
+++ b/solution.py
@@ -18,25 +18,31 @@
 
 HIDDEN_OUT, HIDDEN_IN, CROSS, SELF_OUT, SELF_IN, NORMS = 0, 8, 16, 20, 22, 28
 GROUPS = (
-    (1, 0, 8, (3, 3, 2), 0),
-    (1, 16, 6, (2, 2, 2), 1),
-    (0, 0, 10, (3, 3, 4), 0),
-    (0, 20, 4, (2, 2, 1), 1),
+    (1, 0, 4, (2, 1, 1), 0),
+    (1, 8, 4, (1, 2, 1), 1),
+    (1, 16, 6, (2, 2, 2), 2),
+    (0, 0, 4, (1, 1, 2), 0),
+    (0, 8, 6, (2, 2, 2), 1),
+    (0, 20, 4, (2, 2, 1), 2),
 )
-BANKS = ((3, 3, 4), (2, 2, 2))
+BANKS = ((2, 1, 2), (2, 2, 2), (2, 2, 2))
+FIRST_USERS = 3
 ORDERS = ((0, 1, 2), (1, 2, 0), (2, 0, 1))
-STARTS = (0, 16, 28, 48)
+STARTS = (0, 8, 16, 28, 36, 48)
 SCHEDULE = dict(
-    dec_in3="0s",
-    dec_attend="0b 0a",
-    dec_end="0c",
-    memory_start="1s",
-    enc_in0="0b 0a 0c 1a 1b",
-    enc_in3="2s 1c",
-    enc_start="0b 0c 0a",
-    enc_attend="1c 1b 1a 2a",
-    enc_end="2b 2c 3s",
-    last="1c 1a 3a 0a 2b 3c 2c 1b 3b 2a 1c 0c 3a 3b 3c 2c 2a 2b 3a 3b 3c 0c 2a 2b 0b 1a 2c 1b 3a 3c 3b 1a 0b 1c 1b 2b 2a 0a 3a 2c 3c 3b",
+    dec_in3="1s 0s",
+    dec_start="1b 1a",
+    dec_end="2s 0a 0c 1c",
+    memory_start="0b",
+    memory_end="1a 1b",
+    enc_out="3s 2a",
+    enc_in0="0c 2b",
+    enc_in1="2c",
+    enc_in3="0a 4s 0b",
+    enc_start="1a 1b 0c",
+    enc_attend="2b 2a 2c",
+    enc_end="4b",
+    last="5s 1c 4a 3c 0a 0b 2a 3a 1c 2b 5a 2c 3b 3c 5b 4c 5a 4a 5c 0b 4b 3a 0c 3b 4c 3c 5b 5c 5a 4b 2b 3b 1c 4a 4c 0c 5b 3a 2c 5c 3c 2a 1b 4b 0a 0b 2b 1a 3b 5a 4c 4a 5b 3a 5c 2c 3c 2a 4b 4a 3b 1b 5a 1a 4c 1c 5b 3a 0a 5c",
 )
 PACKED_UNITS = 58
 
@@ -68,7 +74,8 @@
 def attend(query, key, value, bias, shares, context):
     scaled, plain = sides(0.125), sides(1.0)
     heads = [(pair, side) for pair in range(HEADS // 2) for side in range(2)]
-    scores = [dot_nt(query(pair) * scaled[side], key(pair)) + bias[...] for pair, side in heads]
+    masked = bias[...].astype(F32)
+    scores = [dot_nt(query(pair) * scaled[side], key(pair)) + masked for pair, side in heads]
     expvals = [jnp.exp(score - jnp.max(score, -1, keepdims=True)) for score in scores]
     low = [(expval * (1.0 / jnp.sum(expval, -1, keepdims=True))).astype(BF16) for expval in expvals]
     for head in range(HEADS):
@@ -215,31 +222,31 @@
 
 
 class Part:
-    def __init__(self, group, which, first, rows, at):
+    def __init__(self, group, which, first, rows, at, bank_at):
         self.group, self.which, self.first = group, which, first
         self.position, self.order = group.position, ORDERS[which]
-        self.rows = (at, rows)
+        self.rows, self.bank_rows = (at, rows), (bank_at, rows)
 
     def where(self, axis, step):
         return lax.rem(self.position[axis] + (step + 4), 4)
 
     def copy(self, receive, source, target, axis, step):
-        remote(source, target, self.group.send_sems.at[self.which], receive, beside(self.position, axis, step)).start()
+        remote(source, target, self.group.first_sends.at[self.which], receive, beside(self.position, axis, step)).start()
 
     def block(self, step):
         axis = self.order[0]
         return cut(self.group.packed, axis, self.where(axis, step), (self.first, self.rows[1]))
 
     def inbox(self, which, side=None):
-        rows = [pl.ds(*self.rows), slice(None)]
+        rows = [pl.ds(*self.bank_rows), slice(None)]
         middle = [slice(None) if side is None else pl.ds(2 * side, 2), slice(None)]
         return self.group.inbox.at[tuple([which] + middle + rows)]
 
     def outbox(self, side):
-        return self.group.outbox.at[pl.ds(2 * side, 2), :, pl.ds(*self.rows), :]
+        return self.group.outbox.at[pl.ds(2 * side, 2), :, pl.ds(*self.bank_rows), :]
 
     def steps(self):
-        group, axis, rows = self.group, self.order[0], pl.ds(*self.rows)
+        group, axis, rows = self.group, self.order[0], pl.ds(*self.bank_rows)
         far_sem, near_sem = group.far_sems.at[self.which], group.near_sems.at[self.which]
         group.add_swapped(self.which)
         far = self.block(2)
@@ -257,14 +264,21 @@
         landed(group.inbox.at[pl.ds(0, 2), :, :, rows, :], near_sem)
         total = widened(self.block(0)) + widened(self.inbox(0)) + widened(self.inbox(1))
         group.held[0][:, :, self.rows[0] : self.rows[0] + self.rows[1], :] = total.astype(BF16)
-        landed(group.inbox.at[:, :, :, rows, :], group.send_sems.at[self.which])
+        landed(group.inbox.at[:, :, :, rows, :], group.first_sends.at[self.which])
         group.free(self.which)
         self.direct(1)
         yield
         group.held[1][:, self.rows[0] : self.rows[0] + self.rows[1], :] = self.summed(1).astype(BF16)
-        self.direct(2)
+        if group.owner(self.which) is None:
+            self.direct(2)
+        else:
+            pl.when(group.me == group.section)(lambda: self.direct(2))
+            pl.when(group.me != group.section)(self.give)
         yield
-        group.total(self.which, self.summed(2))
+        if group.owner(self.which) is None:
+            group.totals[16 * NORMS : 16 * NORMS + 16, :] = self.summed(2)
+        else:
+            pl.when(group.me == group.section)(self.finish)
         yield
 
     def direct(self, phase):
@@ -272,8 +286,24 @@
         dim = sorted(self.order[phase:]).index(axis)
         held, slots = self.group.held[phase - 1], self.group.slots[phase - 1]
         for i, step in enumerate((2, 1, -1)):
-            remote(cut(held, dim, self.where(axis, step), self.rows), cut(slots, 0, i, self.rows), self.group.send_sems.at[2 + phase],
+            remote(cut(held, dim, self.where(axis, step), self.rows), cut(slots, 0, i, self.rows), self.group.late_sends.at[phase - 1],
                    self.group.direct_sems.at[phase - 1, self.which], beside(self.position, axis, step)).start()
+
+    def give(self):
+        axis = self.order[2]
+        held, slots = self.group.held[1], self.group.slots[2]
+        for i, step in enumerate((2, 1, -1, 0)):
+            remote(cut(held, 0, self.where(axis, step), self.rows), cut(slots, 0, i, self.rows), self.group.late_sends.at[1],
+                   self.group.direct_sems.at[2, self.which], across(self.position, axis, step)).start()
+
+    def finish(self):
+        group = self.group
+        at = 16 * (group.first + self.group.me * group.half) + self.rows[0]
+        group.totals[pl.ds(pl.multiple_of(at, 16), self.rows[1]), :] = self.summed(2)
+        at = 16 * (group.first + (1 - self.group.me) * group.half) + self.rows[0]
+        landed(group.slots[2].at[:, pl.ds(*self.rows), :], group.direct_sems.at[2, self.which])
+        group.totals[pl.ds(pl.multiple_of(at, 16), self.rows[1]), :] = sum(
+            [widened(cut(group.slots[2], 0, i, self.rows)) for i in range(1, 4)], widened(cut(group.slots[2], 0, 0, self.rows)))
 
     def summed(self, phase):
         axis = self.order[phase]
@@ -298,38 +328,45 @@
 
 def group_buffers(units):
     rows = 16 * sum(units)
-    return [pltpu.VMEM(shape + (rows, 128), BF16) for shape in ((4, 4), (4,), (3, 4), (3,))]
+    return [pltpu.VMEM(shape + (rows, 128), BF16) for shape in ((4, 4), (4,), (3, 4), (3,), (4,))]
 
 
 class Group:
     def __init__(self, which, position, packed, arrivals, totals, banks, own, sems, credits):
         self.section, self.first, self.half, self.parts, self.bank = GROUPS[which]
-        self.again, self.reused = which >= 2, which < 2
+        self.again, self.reused = which >= FIRST_USERS, which < FIRST_USERS
         self.position, self.packed, self.totals = position, packed, totals
         self.me = lax.axis_index("section")
-        self.swap_sems, self.far_sems, self.near_sems, self.direct_sems, self.send_sems, self.total_sems = sems
+        self.swap_sems, self.far_sems, self.near_sems, self.first_sends, self.direct_sems, self.late_sends = sems
         self.swap_credit, self.part_credit = credits
         self.units = sum(self.parts)
         rows = 16 * self.units
         self.arrival = arrivals[self.bank]
         self.inbox, self.outbox = banks[self.bank]
-        self.inbox = self.inbox.at[:, :, :, pl.ds(0, rows), :]
         self.held, self.slots = own[:2], own[2:]
         self.offsets = [sum(self.parts[:i]) for i in range(3)]
+        self.bank_offsets = [sum(BANKS[self.bank][:i]) for i in range(3)]
         self.start, self.other = [
             pl.multiple_of(16 * STARTS[which] + side * rows, 16) for side in (self.me, 1 - self.me)
         ]
-        self.work = [Part(self, i, self.start + 16 * self.offsets[i], 16 * self.parts[i], 16 * self.offsets[i]) for i in range(3)]
+        self.work = [
+            Part(self, i, self.start + 16 * self.offsets[i], 16 * self.parts[i], 16 * self.offsets[i], 16 * self.bank_offsets[i])
+            for i in range(3)
+        ]
+
+    def owner(self, i):
+        return self.section if self.offsets[i] < self.half else None
 
     def swap(self, i):
         rows = 16 * self.parts[i]
         source = self.packed.at[:, :, :, pl.ds(self.other + 16 * self.offsets[i], rows), :]
-        target = self.arrival.at[:, :, :, pl.ds(16 * self.offsets[i], rows), :]
+        target = self.arrival.at[:, :, :, pl.ds(16 * self.bank_offsets[i], rows), :]
         return remote(source, target, self.swap_sems.at[3], self.swap_sems.at[i], partner())
 
     def start_swap(self):
-        self.begun = self.ended = 0
+        self.begun = 0
         if self.again:
+            self.before.swapped()
             pl.semaphore_wait(self.swap_credit, 1)
         for i in range(3):
             self.swap(i).start()
@@ -339,7 +376,7 @@
         part = self.work[i]
         self.swap(i).wait_recv()
         mine = self.packed.at[:, :, :, pl.ds(part.first, part.rows[1]), :]
-        mine[...] = mine[...] + self.arrival[:, :, :, part.rows[0] : part.rows[0] + part.rows[1], :]
+        mine[...] = mine[...] + self.arrival[:, :, :, part.bank_rows[0] : part.bank_rows[0] + part.rows[1], :]
         self.begun += 1
         if self.reused and self.begun == 3:
             pl.semaphore_signal(self.swap_credit, inc=1, device_id=partner(), device_id_type=MESH)
@@ -351,36 +388,26 @@
             for step in (1, -1):
                 pl.semaphore_signal(self.part_credit.at[i], inc=1, device_id=beside(self.position, ORDERS[i][0], step), device_id_type=MESH)
 
-    def total(self, i, total):
-        base = 16 * (self.first + self.me * self.half)
-        if self.offsets[i] < self.half:
-            at = pl.multiple_of(base + 16 * self.offsets[i], 16)
-            self.totals[self.section, pl.ds(at, 16 * self.parts[i]), :] = total
-        else:
-            self.totals[self.me, 16 * NORMS : 16 * NORMS + 16, :] = total
-        self.ended += 1
-        if self.ended < 3:
-            return
-        mine = self.totals.at[self.section, pl.ds(pl.multiple_of(base, 16), 16 * self.half), :]
-        self.handed = remote(mine, mine, self.total_sems.at[0], self.total_sems.at[1], partner())
+    def swapped(self):
+        landed(self.packed.at[:, :, :, pl.ds(self.other, 16 * self.units), :], self.swap_sems.at[3])
+
+    def close(self):
+        if self.again:
+            self.swapped()
+        landed(self.slots[0], self.late_sends.at[0])
+        given = 16 * self.half
+        rest = 16 * self.units - given
+
+        @pl.when(self.me == self.section)
+        def _():
+            landed(self.slots[1], self.late_sends.at[1])
 
         @pl.when(self.me != self.section)
         def _():
-            self.handed.start()
-
-    def close(self):
-        landed(self.packed.at[:, :, :, pl.ds(self.other, 16 * self.units), :], self.swap_sems.at[3])
-        landed(self.slots[0], self.send_sems.at[3])
-        landed(self.slots[1], self.send_sems.at[4])
-        theirs = pl.multiple_of(16 * (self.first + (1 - self.me) * self.half), 16)
-
-        @pl.when(self.me != self.section)
-        def _():
-            self.handed.wait_send()
-
-        @pl.when(self.me == self.section)
-        def _():
-            landed(self.totals.at[self.section, pl.ds(theirs, 16 * self.half), :], self.total_sems.at[1])
+            if rest:
+                landed(self.packed.at[0, 0, 0, pl.ds(0, 4 * given + 3 * rest), :], self.late_sends.at[1])
+            else:
+                landed(self.slots[2], self.late_sends.at[1])
 
 
 def keep_attention():
@@ -388,7 +415,7 @@
 
 
 def keep_norm():
-    return [pltpu.VMEM((256, 512), F32), pltpu.VMEM((256, 1), F32)]
+    return [pltpu.VMEM((256, 512), F32)]
 
 
 def keep_ffn():
@@ -400,16 +427,17 @@
 
 
 def scratch_shapes():
-    low, wide, square = pltpu.VMEM((256, 512), BF16), pltpu.VMEM((256, 512), F32), pltpu.VMEM((256, 256), F32)
+    low, wide, square = pltpu.VMEM((256, 512), BF16), pltpu.VMEM((256, 512), F32), pltpu.VMEM((256, 256), BF16)
     return dict(
         weights=stacked([pltpu.VMEM(shape, BF16) for shape in WEIGHTS]),
         inputs=stacked([low, low, pltpu.VMEM((6, 1, 512), F32)]),
-        selfs=stacked(keep_attention() + keep_norm()),
+        selfs=stacked(keep_attention() + keep_norm() + [pltpu.VMEM((256, 1), F32)]),
+        scales=pltpu.VMEM((256, 128), F32),
         firsts=stacked([low, wide]),
-        enc=keep_ffn()[1:] + keep_norm() + keep_norm() + [low, pltpu.VMEM((256, 1024), BF16)],
+        enc=keep_ffn()[1:] + keep_norm() + keep_norm() + [pltpu.VMEM((256, 1024), BF16)],
         cross=[low, pltpu.VMEM((8, 256, 256), BF16), low] + keep_norm(),
         dec=keep_ffn() + keep_norm(),
-        bias=[pltpu.VMEM((2, 256, 256), F32), square],
+        bias=[pltpu.VMEM((2, 256, 256), BF16), square],
         work=[wide, low, pltpu.VMEM((8, 512), F32)],
         results=[low, low],
         packed=pltpu.VMEM((4, 4, 4, 16 * PACKED_UNITS, 128), BF16),
@@ -417,17 +445,18 @@
         banks=[bank_buffers(units) for units in BANKS],
         groups=[group_buffers(group[3]) for group in GROUPS],
         places=[pltpu.VMEM((2, 1, ROW), jnp.int32), pltpu.SMEM((2, 1, NSEG), jnp.int32)],
-        totals=pltpu.VMEM((2, 464, 128), F32),
+        totals=pltpu.VMEM((464, 128), F32),
         in_sems=pltpu.SemaphoreType.DMA((2, 8)),
         in_sends=pltpu.SemaphoreType.DMA((8,)),
         place_sems=pltpu.SemaphoreType.DMA((2,)),
         out_sems=pltpu.SemaphoreType.DMA((3, 2)),
         group_sems=[
-            [pltpu.SemaphoreType.DMA(shape) for shape in ((4,), (3,), (3,), (2, 3), (5,), (2,))]
+            [pltpu.SemaphoreType.DMA(shape) for shape in ((3, 3), (2,))]
             for _ in GROUPS
         ],
-        swap_credit=pltpu.SemaphoreType.REGULAR((2,)),
-        part_credit=pltpu.SemaphoreType.REGULAR((2, 3)),
+        bank_sems=[[pltpu.SemaphoreType.DMA(shape) for shape in ((4,), (3,), (3,), (3,))] for _ in BANKS],
+        swap_credit=pltpu.SemaphoreType.REGULAR((3,)),
+        part_credit=pltpu.SemaphoreType.REGULAR((3, 3)),
     )
 
 
@@ -472,6 +501,31 @@
         copy.start()
     for i in (5, 0, 7, 1, 3, 4, 2, 6):
         local(i).start()
+
+    pl.semaphore_wait(barrier, 13)
+    for i in (5, 7, 0, 1):
+        sent(i).start()
+    def pieces(i):
+        first = 0
+        for k, rows in enumerate((352, 352, 336, 336, 336, 336)):
+            piece = pl.ds(first, rows)
+            remote(own[i].at[0, piece], held[i].at[me, piece], s["in_sends"].at[i], s["in_sems"].at[me, i],
+                   across(position, k // 2, 1 - 2 * (k % 2))).start()
+            first += rows
+
+    @pl.when(me == 0)
+    def _():
+        pieces(4)
+        for i in (3, 2):
+            sent(i).start()
+
+    @pl.when(me != 0)
+    def _():
+        for i in (2, 3):
+            sent(i).start()
+
+    sent(6).start()
+
     for copy in places:
         copy.wait()
 
@@ -487,31 +541,9 @@
     target_row = segments[me].astype(F32)
     target_col = jnp.broadcast_to(target_row, (128, ROW)).T[:, 0:1]
     ids_row, ids_col = ids_row.astype(F32), ids_col.astype(F32)
-    bias[0] = jnp.where(ids_col == ids_row, 0.0, -1e30)
-    bias[1] = jnp.where(target_col == target_row, 0.0, -1e30)
-    cross_bias[...] = jnp.where(target_col == ids_row, 0.0, -1e30)
-
-    pl.semaphore_wait(barrier, 13)
-    for i in (5, 7, 0, 1):
-        sent(i).start()
-    first = 0
-    for k, rows in enumerate((352, 352, 336, 336, 336, 336)):
-        piece = pl.ds(first, rows)
-        remote(own[4].at[0, piece], held[4].at[me, piece], s["in_sends"].at[4], s["in_sems"].at[me, 4],
-               across(position, k // 2, 1 - 2 * (k % 2))).start()
-        first += rows
-
-    @pl.when(me == 0)
-    def _():
-        for i in (3, 2):
-            sent(i).start()
-
-    @pl.when(me != 0)
-    def _():
-        for i in (2, 3):
-            sent(i).start()
-
-    sent(6).start()
+    bias[0] = jnp.where(ids_col == ids_row, 0.0, -1e30).astype(BF16)
+    bias[1] = jnp.where(target_col == target_row, 0.0, -1e30).astype(BF16)
+    cross_bias[...] = jnp.where(target_col == ids_row, 0.0, -1e30).astype(BF16)
 
     w_self_in, w_self_out, w_cross, w_in, w_out = s["weights"]
     x, cot, norms = s["inputs"]
@@ -524,6 +556,10 @@
         j = lax.rem(me + i, 2)
         for which in (5, 0, 7, 1):
             ready(j, which)
+        @pl.when((me != 0) & (i == 1))
+        def _():
+            pieces(4)
+
         projected, shares, context, normed, scale = [ref.at[j] for ref in s["selfs"]]
         result = self_forward(x.at[j], w_self_in.at[j], w_self_out.at[j], bias.at[j], norms.at[j], projected, shares, context, normed, scale)
         first[j] = result
@@ -532,9 +568,10 @@
 
     lax.fori_loop(0, 2, self_block, 0)
 
-    enc_active, enc_slopes, enc_normed, enc_scale, memory_normed, memory_scale, memory_keep, key_value = s["enc"]
-    queries, cross_shares, cross_context, cross_normed, cross_scale = s["cross"]
-    dec_low, dec_active, dec_slopes, dec_normed, dec_scale = s["dec"]
+    enc_active, enc_slopes, enc_normed, memory_normed, key_value = s["enc"]
+    queries, cross_shares, cross_context, cross_normed = s["cross"]
+    dec_low, dec_active, dec_slopes, dec_normed = s["dec"]
+    enc_scale, memory_scale, cross_scale, dec_scale = [s["scales"].at[:, i : i + 1] for i in range(4)]
     enc_self, dec_self = [ref.at[0] for ref in s["selfs"]], [ref.at[1] for ref in s["selfs"]]
     enc_norms, dec_norms = norms.at[0], norms.at[1]
 
@@ -578,10 +615,13 @@
 
     packed = s["packed"]
     groups = [
-        Group(g, position, packed, s["arrivals"], s["totals"], s["banks"], s["groups"][g], s["group_sems"][g],
+        Group(g, position, packed, s["arrivals"], s["totals"], s["banks"], s["groups"][g], s["bank_sems"][GROUPS[g][4]] + s["group_sems"][g],
               (s["swap_credit"].at[GROUPS[g][4]], s["part_credit"].at[GROUPS[g][4]]))
-        for g in range(4)
+        for g in range(len(GROUPS))
     ]
+    for group in groups[FIRST_USERS:]:
+        group.before = next(other for other in groups if other.bank == group.bank)
+
     def at(moment, which=None):
         for step in SCHEDULE.get(moment if which is None else moment + str(which), "").split():
             group = groups[int(step[0])]
@@ -593,12 +633,12 @@
     def ffn_back(gradient, low, section, activated, slopes, moment):
         result = gradient.astype(BF16)
         for i in range(4):
+            pack_tall(packed, section, i, dot_tn(activated[:, 512 * i : 512 * i + 512], result))
+        at(moment + "_out")
+        for i in range(4):
             rows = slice(512 * i, 512 * i + 512)
             slopes[:, rows] = (dot_nt(result, w_out[section, rows, :]) * slopes[:, rows].astype(F32)).astype(BF16)
-            pack_tall(packed, section, i, dot_tn(activated[:, rows], result))
-            at(moment + "_out", i)
-        for i in range(4):
-            pack(packed, section, HIDDEN_IN + 2 * i, dot_tn(low[...], slopes[:, 512 * i : 512 * i + 512]))
+            pack(packed, section, HIDDEN_IN + 2 * i, dot_tn(low[...], slopes[:, rows]))
             at(moment + "_in", i)
         return dot_nt(slopes[...], w_in[section])
 
@@ -666,7 +706,7 @@
 
     for group in groups:
         group.close()
-    copy = pltpu.make_async_copy(s["totals"].at[me], totals_out, s["place_sems"].at[0])
+    copy = pltpu.make_async_copy(s["totals"], totals_out, s["place_sems"].at[0])
     copy.start()
     for i in range(8):
         sent(i).wait_send()

time: 72.4 us -> 68.9 us (0.952); the launches traced: 70.9 us -> 68.7 us
  Pallas kernels: 70.3 us -> 68 us
    pallas_call x1, Pallas kernels: 67.6 us -> 65.3 us  [body(): pl.pallas_call(lambda *refs: whole_kernel(tree, *refs), out_shape=large +...]
where the time goes in v3:
time: 68.9 us; the launch traced here: 68.7 us
  Pallas kernels  68 us (99%)
    pallas_call x1, Pallas kernels, body(): pl.pallas_call(lambda *refs: whole_kernel(tree, *refs), out_shape=large +...  65.3 us
    pallas_call x1, Pallas kernels, body(): pl.pallas_call(finish_kernel, out_shape=large + [jax.ShapeDtypeStruct(sha...  2.69 us

profile of v3, /device:TPU:0, one launch (start us, length us, event | category | flops | bytes accessed | tf_op | source)
XLA Modules:
  0.0 68.7 jit_solution(4195818663749058114)
XLA Ops:
  0.6 65.3 %layer_pair.1 = (bf16[1,2,1,256,512]{4,3,2,1,0:T(8,128)(2,1)}, f32[1,2,1,256,512]{4,3,2,1,0:T(8,128)}, f32[464,128]{1,0:T(8,128)}) custom-call(bf16[1,2,1,256,512]{4,3,2,1,0:T(8,128)(2,1)} %refs_0_.1, bf16[1,2,1,256,512]{4,3,2,1,0:T(8,128)(2,1)} %refs_1_.1, s32[2,1,8]{2,1,0:T(1,128)} %refs_2_.1, s32[2,1,256]{2,1,0:T(1,128)} %refs_3_.1, ...), custom_call_target="tpu_custom_call" | custom-call | tf_op jit(solution)/shard_map/layer_pair/pallas_call | solution.py:741
  66.0 2.7 %finish.1 = (bf16[1,2,1,256,512]{4,3,2,1,0:T(8,128)(2,1)}, f32[1,2,1,256,512]{4,3,2,1,0:T(8,128)}, f32[1,8,1536]{2,1,0:T(8,128)}, f32[1,8,512]{2,1,0:T(8,128)}, ...) custom-call(bf16[1,2,1,256,512]{4,3,2,1,0:T(8,128)(2,1)} %get-tuple-element.19.layer_, ...), custom_call_target="tpu_custom_call" | custom-call | tf_op jit(solution)/shard_map/finish/pallas_call | solution.py:752

commit v4 on v3

--- a/solution.py
+++ b/solution.py
@@ -163,9 +163,12 @@
     return columns_of(ref, 0), columns_of(ref, 512), columns_of(ref, 1024)
 
 
-def self_forward(inputs, self_in, self_out, bias, params, projected, shares, context, normed, scale):
+def project(inputs, self_in, projected):
     for i in range(3):
         projected[:, 512 * i : 512 * i + 512] = dot(inputs[...], self_in[:, 512 * i : 512 * i + 512]).astype(BF16)
+
+
+def self_forward(inputs, self_out, bias, params, projected, shares, context, normed, scale):
     attend(*thirds(projected), bias, shares, context)
     return norm(inputs[...].astype(F32) + dot(context[...], self_out[...]), params, 0, normed, scale)
 
@@ -448,7 +451,8 @@
         totals=pltpu.VMEM((464, 128), F32),
         in_sems=pltpu.SemaphoreType.DMA((2, 8)),
         in_sends=pltpu.SemaphoreType.DMA((8,)),
-        place_sems=pltpu.SemaphoreType.DMA((2,)),
+        place_sems=pltpu.SemaphoreType.DMA((3,)),
+        project_sems=pltpu.SemaphoreType.DMA((2,)),
         out_sems=pltpu.SemaphoreType.DMA((3, 2)),
         group_sems=[
             [pltpu.SemaphoreType.DMA(shape) for shape in ((3, 3), (2,))]
@@ -497,14 +501,17 @@
 
     segments, lengths = s["places"]
     places = [pltpu.make_async_copy((segments_in, lengths_in)[i], s["places"][i], s["place_sems"].at[i]) for i in range(2)]
+    others = pltpu.make_async_copy(given(5, 1 - me), s["dec"][0], s["place_sems"].at[2])
     for copy in places:
         copy.start()
-    for i in (5, 0, 7, 1, 3, 4, 2, 6):
+    others.start()
+    for i in (0, 5, 7, 1, 3, 4, 2, 6):
         local(i).start()
 
     pl.semaphore_wait(barrier, 13)
-    for i in (5, 7, 0, 1):
+    for i in (5, 7, 1):
         sent(i).start()
+
     def pieces(i):
         first = 0
         for k, rows in enumerate((352, 352, 336, 336, 336, 336)):
@@ -516,15 +523,7 @@
     @pl.when(me == 0)
     def _():
         pieces(4)
-        for i in (3, 2):
-            sent(i).start()
-
-    @pl.when(me != 0)
-    def _():
-        for i in (2, 3):
-            sent(i).start()
-
-    sent(6).start()
+
 
     for copy in places:
         copy.wait()
@@ -552,21 +551,35 @@
     memory_low, third_low = s["results"]
     source_grad, target_grad = first.at[0], first.at[1]
 
-    def self_block(i, carry):
+    others.wait()
+    ready(me, 0)
+    staged = s["enc"][0].at[:, pl.ds(0, 1536)]
+    project(s["dec"][0], w_self_in.at[me], staged)
+    given_projection = remote(staged, s["selfs"][0].at[me], s["project_sems"].at[0], s["project_sems"].at[1], partner())
+    given_projection.start()
+
+    @pl.when(me == 0)
+    def _():
+        for i in (3, 2, 6, 0):
+            sent(i).start()
+
+    @pl.when(me != 0)
+    def _():
+        for i in (2, 3, 4, 6, 0):
+            sent(i).start()
+
+    for i in range(2):
         j = lax.rem(me + i, 2)
-        for which in (5, 0, 7, 1):
+        for which in (5, 7, 1):
             ready(j, which)
-        @pl.when((me != 0) & (i == 1))
-        def _():
-            pieces(4)
-
         projected, shares, context, normed, scale = [ref.at[j] for ref in s["selfs"]]
-        result = self_forward(x.at[j], w_self_in.at[j], w_self_out.at[j], bias.at[j], norms.at[j], projected, shares, context, normed, scale)
+        if i == 0:
+            project(x.at[j], w_self_in.at[j], projected)
+        else:
+            landed(projected, s["project_sems"].at[1])
+        result = self_forward(x.at[j], w_self_out.at[j], bias.at[j], norms.at[j], projected, shares, context, normed, scale)
         first[j] = result
         first_low[j] = result.astype(BF16)
-        return carry
-
-    lax.fori_loop(0, 2, self_block, 0)
 
     enc_active, enc_slopes, enc_normed, memory_normed, key_value = s["enc"]
     queries, cross_shares, cross_context, cross_normed = s["cross"]
@@ -575,6 +588,7 @@
     enc_self, dec_self = [ref.at[0] for ref in s["selfs"]], [ref.at[1] for ref in s["selfs"]]
     enc_norms, dec_norms = norms.at[0], norms.at[1]
 
+    given_projection.wait_send()
     result = ffn_forward(first_low.at[0], w_in.at[0], w_out.at[0], enc_active, enc_slopes, lambda: ready(0, 3), lambda: ready(0, 4))
     second = norm(first[0] + result, enc_norms, 1, enc_normed, enc_scale)
     memory = norm(second, enc_norms, 2, memory_normed, memory_scale).astype(BF16)
@@ -638,7 +652,8 @@
         for i in range(4):
             rows = slice(512 * i, 512 * i + 512)
             slopes[:, rows] = (dot_nt(result, w_out[section, rows, :]) * slopes[:, rows].astype(F32)).astype(BF16)
-            pack(packed, section, HIDDEN_IN + 2 * i, dot_tn(low[...], slopes[:, rows]))
+        for i in range(4):
+            pack(packed, section, HIDDEN_IN + 2 * i, dot_tn(low[...], slopes[:, 512 * i : 512 * i + 512]))
             at(moment + "_in", i)
         return dot_nt(slopes[...], w_in[section])
 
@@ -682,6 +697,7 @@
     self_back_b(1, dec_self, "dec")
     self_back_c(1, dec_self)
     at("dec_end")
+    pl.when(me != 1)(lambda: ready(1, 0))
     target_grad[...] = work[...] + dot_nt(dec_self[0][...], w_self_in[1])
 
     for i in range(2):
@@ -700,6 +716,7 @@
     self_back_b(0, enc_self, "enc")
     self_back_c(0, enc_self)
     at("enc_end")
+    pl.when(me != 0)(lambda: ready(0, 0))
     source_grad[...] = work[...] + dot_nt(enc_self[0][...], w_self_in[0])
     put_out(1, token_grads, (source_grad, target_grad))
     at("last")

time: 68.9 us -> 68.4 us (level)
  no operation moved by 1% of the time
where the time goes in v4:
time: 68.4 us; the launch traced here: 68.2 us
  Pallas kernels  67.6 us (99%)
    pallas_call x1, Pallas kernels, body(): pl.pallas_call(lambda *refs: whole_kernel(tree, *refs), out_shape=large +...  64.9 us
    pallas_call x1, Pallas kernels, body(): pl.pallas_call(finish_kernel, out_shape=large + [jax.ShapeDtypeStruct(sha...  2.69 us

profile of v4, /device:TPU:0, one launch (start us, length us, event | category | flops | bytes accessed | tf_op | source)
XLA Modules:
  0.0 68.2 jit_solution(1427866806228601148)
XLA Ops:
  0.6 64.9 %layer_pair.1 = (bf16[1,2,1,256,512]{4,3,2,1,0:T(8,128)(2,1)}, f32[1,2,1,256,512]{4,3,2,1,0:T(8,128)}, f32[464,128]{1,0:T(8,128)}) custom-call(bf16[1,2,1,256,512]{4,3,2,1,0:T(8,128)(2,1)} %refs_0_.1, bf16[1,2,1,256,512]{4,3,2,1,0:T(8,128)(2,1)} %refs_1_.1, s32[2,1,8]{2,1,0:T(1,128)} %refs_2_.1, s32[2,1,256]{2,1,0:T(1,128)} %refs_3_.1, ...), custom_call_target="tpu_custom_call" | custom-call | tf_op jit(solution)/shard_map/layer_pair/pallas_call | solution.py:758
  65.5 2.7 %finish.1 = (bf16[1,2,1,256,512]{4,3,2,1,0:T(8,128)(2,1)}, f32[1,2,1,256,512]{4,3,2,1,0:T(8,128)}, f32[1,8,1536]{2,1,0:T(8,128)}, f32[1,8,512]{2,1,0:T(8,128)}, ...) custom-call(bf16[1,2,1,256,512]{4,3,2,1,0:T(8,128)(2,1)} %get-tuple-element.19.layer_, ...), custom_call_target="tpu_custom_call" | custom-call | tf_op jit(solution)/shard_map/finish/pallas_call | solution.py:769

commit v5 on v4

--- a/solution.py
+++ b/solution.py
@@ -450,7 +450,7 @@
         places=[pltpu.VMEM((2, 1, ROW), jnp.int32), pltpu.SMEM((2, 1, NSEG), jnp.int32)],
         totals=pltpu.VMEM((464, 128), F32),
         in_sems=pltpu.SemaphoreType.DMA((2, 8)),
-        in_sends=pltpu.SemaphoreType.DMA((8,)),
+        in_sends=pltpu.SemaphoreType.DMA((2,)),
         place_sems=pltpu.SemaphoreType.DMA((3,)),
         project_sems=pltpu.SemaphoreType.DMA((2,)),
         out_sems=pltpu.SemaphoreType.DMA((3, 2)),
@@ -494,7 +494,7 @@
         return pltpu.make_async_copy(given(i, me), held[i].at[me], s["in_sems"].at[me, i])
 
     def sent(i):
-        return remote(given(i, 1 - me), held[i].at[me], s["in_sends"].at[i], s["in_sems"].at[me, i], partner())
+        return remote(given(i, 1 - me), held[i].at[me], s["in_sends"].at[1 if i == 7 else 0], s["in_sems"].at[me, i], partner())
 
     def ready(j, i):
         pltpu.make_async_copy(given(i, 0), held[i].at[j], s["in_sems"].at[j, i]).wait()
@@ -516,7 +516,7 @@
         first = 0
         for k, rows in enumerate((352, 352, 336, 336, 336, 336)):
             piece = pl.ds(first, rows)
-            remote(own[i].at[0, piece], held[i].at[me, piece], s["in_sends"].at[i], s["in_sems"].at[me, i],
+            remote(own[i].at[0, piece], held[i].at[me, piece], s["in_sends"].at[1 if i == 7 else 0], s["in_sems"].at[me, i],
                    across(position, k // 2, 1 - 2 * (k % 2))).start()
             first += rows
 
@@ -721,12 +721,12 @@
     put_out(1, token_grads, (source_grad, target_grad))
     at("last")
 
+    copy = pltpu.make_async_copy(s["totals"], totals_out, s["place_sems"].at[0])
+    copy.start()
     for group in groups:
         group.close()
-    copy = pltpu.make_async_copy(s["totals"], totals_out, s["place_sems"].at[0])
-    copy.start()
-    for i in range(8):
-        sent(i).wait_send()
+    landed(packed.at[:, :, :, pl.ds(0, 480), :], s["in_sends"].at[0])
+    sent(7).wait_send()
     out_done(0, layer_out, (memory_low, third_low))
     out_done(1, token_grads, (source_grad, target_grad))
     copy.wait()

time: 68.4 us -> 68.3 us (level)
  no operation moved by 1% of the time
where the time goes in v5:
time: 68.3 us; the launch traced here: 68.2 us
  Pallas kernels  67.5 us (99%)
    pallas_call x1, Pallas kernels, body(): pl.pallas_call(lambda *refs: whole_kernel(tree, *refs), out_shape=large +...  64.8 us
    pallas_call x1, Pallas kernels, body(): pl.pallas_call(finish_kernel, out_shape=large + [jax.ShapeDtypeStruct(sha...  2.69 us

profile of v5, /device:TPU:0, one launch (start us, length us, event | category | flops | bytes accessed | tf_op | source)
XLA Modules:
  0.0 68.2 jit_solution(2893945746367718365)
XLA Ops:
  0.6 64.8 %layer_pair.1 = (bf16[1,2,1,256,512]{4,3,2,1,0:T(8,128)(2,1)}, f32[1,2,1,256,512]{4,3,2,1,0:T(8,128)}, f32[464,128]{1,0:T(8,128)}) custom-call(bf16[1,2,1,256,512]{4,3,2,1,0:T(8,128)(2,1)} %refs_0_.1, bf16[1,2,1,256,512]{4,3,2,1,0:T(8,128)(2,1)} %refs_1_.1, s32[2,1,8]{2,1,0:T(1,128)} %refs_2_.1, s32[2,1,256]{2,1,0:T(1,128)} %refs_3_.1, ...), custom_call_target="tpu_custom_call" | custom-call | tf_op jit(solution)/shard_map/layer_pair/pallas_call | solution.py:758
  65.5 2.7 %finish.1 = (bf16[1,2,1,256,512]{4,3,2,1,0:T(8,128)(2,1)}, f32[1,2,1,256,512]{4,3,2,1,0:T(8,128)}, f32[1,8,1536]{2,1,0:T(8,128)}, f32[1,8,512]{2,1,0:T(8,128)}, ...) custom-call(bf16[1,2,1,256,512]{4,3,2,1,0:T(8,128)(2,1)} %get-tuple-element.19.layer_, ...), custom_call_target="tpu_custom_call" | custom-call | tf_op jit(solution)/shard_map/finish/pallas_call | solution.py:769
